TPU v7x, 32 devices: a whole 2x2x4 slice. The times are simulated.
32 devices in a mesh: dp: 8 (over z, x), tensor: 4 (over y, core).
Axes of the slice: x: 2, y: 2, z: 4, core: 2. Of those that a mesh axis runs over, the one named last changes fastest.
Arguments:
- tokens: bfloat16 [14336, 768], P('dp'), may hold values from -6 to 6
- clip_starts: int32 [16, 4], P('dp'), may hold values from 0 to 896, as said below
- cls_index: int32 [16, 4], P('dp'), may hold values from 0 to 896, as said below
- norm_gains: bfloat16 [2, 768], replicated, may hold values from 0.5 to 1.5
- shifts: bfloat16 [4, 768], replicated, may hold values from -3 to 3
- qkv_weight: bfloat16 [768, 3, 768], P(None, None, 'tensor'), may hold values from -0.3125 to 0.3125
- qv_bias: bfloat16 [2, 768], P(None, 'tensor'), may hold values from -3 to 3
- out_weight: bfloat16 [768, 768], P('tensor'), may hold values from -0.625 to 0.625
- fc1_weight: bfloat16 [768, 3072], P(None, 'tensor'), may hold values from -0.21875 to 0.21875
- fc1_bias: bfloat16 [3072], P('tensor'), may hold values from -3 to 3
- fc2_weight: bfloat16 [3072, 768], P('tensor'), may hold values from -0.15625 to 0.15625
- cotangent: bfloat16 [14336, 768], P('dp'), may hold values from -6 to 6
Outputs:
- layer_out: bfloat16 [14336, 768], P('dp')
- input_grad: bfloat16 [14336, 768], P('dp')
- norm_gain_grad: float32 [2, 768], replicated
- shift_grad: float32 [4, 768], replicated
- qkv_grad: float32 [768, 3, 768], P(None, None, 'tensor')
- qv_bias_grad: float32 [2, 768], P(None, 'tensor')
- out_weight_grad: float32 [768, 768], P('tensor')
- fc1_weight_grad: float32 [768, 3072], P(None, 'tensor')
- fc1_bias_grad: float32 [3072], P('tensor')
- fc2_weight_grad: float32 [3072, 768], P('tensor')
Inputs may be any that keep to these rules, and one draw needn't show every extreme that they name: `clip_starts`: row s gives where the clips of sequence s begin: entry 0 is 0, the entries below 896 rise strictly, and entries equal to 896 mark absent clips; every sequence has two to four clips. `cls_index`: entry c is the position of clip c's CLS token in its sequence, inside clip c; 896 where clip c is absent.
All inputs are finite; a program needn't handle non-finite values.
Results may differ from a plain program's by a relative error of at most 0.019.
Values may be sent and summed in bfloat16 or wider, within the bound.
A program may use at most 192 MiB of HBM per device.

v0:
```python
import jax
import jax.numpy as jnp
from jax import lax
from jax.sharding import PartitionSpec as P

HEAD_DIM = 64
LENGTH = 896


def normalize(values):
    centre = values - jnp.mean(values, axis=-1, keepdims=True)
    factor = lax.rsqrt(jnp.mean(centre * centre, axis=-1, keepdims=True) + 1e-06)
    return (centre * factor, factor)


def norm_back(grad_rows, scaled, factor, gain_row):
    inner_grad = grad_rows * gain_row
    return factor * (
        inner_grad
        - jnp.mean(inner_grad, axis=-1, keepdims=True)
        - scaled * jnp.mean(inner_grad * scaled, axis=-1, keepdims=True)
    )


def visible(starts, marks):
    position = jnp.arange(LENGTH, dtype=jnp.int32)
    clip_of = jnp.sum((position[:, None] >= starts[None, :]).astype(jnp.int32), axis=1) - 1
    marked = jnp.any(position[:, None] == marks[None, :], axis=1)
    return (clip_of[:, None] == clip_of[None, :]) | marked[None, :]


def contract_rows(left, right):
    return lax.dot_general(
        left, right, (((0,), (0,)), ((), ())), preferred_element_type=jnp.float32
    )


def contract_cols(left, right):
    return lax.dot_general(
        left, right, (((1,), (1,)), ((), ())), preferred_element_type=jnp.float32
    )


def raw_scores(queries, key_rows, allowed):
    scores = (
        jnp.einsum("qhd,khd->hqk", queries, key_rows, preferred_element_type=jnp.float32) * 0.125
    )
    return jnp.where(allowed[None], scores, -1e30)


def attend(pieces):
    queries, key_rows, value_rows, allowed = pieces
    scores = raw_scores(queries, key_rows, allowed)
    row_max = jnp.max(scores, axis=-1, keepdims=True)
    exponent = jnp.exp(scores - row_max)
    totals = jnp.sum(exponent, axis=-1, keepdims=True)
    attn_prob = exponent / totals
    context = jnp.einsum(
        "hqk,khd->qhd",
        attn_prob.astype(jnp.bfloat16),
        value_rows,
        preferred_element_type=jnp.float32,
    )
    return (context.astype(jnp.bfloat16), (row_max + jnp.log(totals))[..., 0])


def attend_back(pieces):
    queries, key_rows, value_rows, allowed, log_total, grad_context = pieces
    scores = raw_scores(queries, key_rows, allowed)
    attn_prob = jnp.where(allowed[None], jnp.exp(scores - log_total[..., None]), 0.0)
    grad_prob = jnp.einsum(
        "qhd,khd->hqk", grad_context, value_rows, preferred_element_type=jnp.float32
    )
    grad_value = jnp.einsum(
        "hqk,qhd->khd",
        attn_prob.astype(jnp.bfloat16),
        grad_context,
        preferred_element_type=jnp.float32,
    )
    grad_score = attn_prob * (grad_prob - jnp.sum(attn_prob * grad_prob, axis=-1, keepdims=True))
    grad_score = grad_score.astype(jnp.bfloat16)
    grad_query = (
        jnp.einsum("hqk,khd->qhd", grad_score, key_rows, preferred_element_type=jnp.float32) * 0.125
    )
    grad_key = (
        jnp.einsum("hqk,qhd->khd", grad_score, queries, preferred_element_type=jnp.float32) * 0.125
    )
    return (
        grad_query.astype(jnp.bfloat16),
        grad_key.astype(jnp.bfloat16),
        grad_value.astype(jnp.bfloat16),
    )


def front_part(tokens, masks, norm_gains, shifts, qkv_weight, qv_bias, out_weight):
    inputs = tokens.astype(jnp.float32)
    scaled_one, factor_one = normalize(inputs)
    normed_one = (
        scaled_one * norm_gains[0].astype(jnp.float32) + shifts[0].astype(jnp.float32)
    ).astype(jnp.bfloat16)
    projected = jnp.einsum(
        "td,dce->tce", normed_one, qkv_weight, preferred_element_type=jnp.float32
    )
    qv_float = qv_bias.astype(jnp.float32)
    local_width = projected.shape[2]
    seq_shape = (masks.shape[0], LENGTH, local_width // HEAD_DIM, HEAD_DIM)
    queries = (projected[:, 0] + qv_float[0]).astype(jnp.bfloat16).reshape(seq_shape)
    key_rows = projected[:, 1].astype(jnp.bfloat16).reshape(seq_shape)
    value_rows = (projected[:, 2] + qv_float[1]).astype(jnp.bfloat16).reshape(seq_shape)
    context, log_total = lax.map(attend, (queries, key_rows, value_rows, masks))
    context = context.reshape(tokens.shape[0], local_width)
    partial_value = jnp.dot(context, out_weight, preferred_element_type=jnp.float32)
    return (
        inputs,
        scaled_one,
        factor_one,
        normed_one,
        queries,
        key_rows,
        value_rows,
        context,
        log_total,
        partial_value,
    )


def middle_part(inputs, attn_total, norm_gains, shifts, fc1_weight, fc1_bias):
    mixed = inputs + attn_total + shifts[2].astype(jnp.float32)
    scaled_two, factor_two = normalize(mixed)
    normed_two = (
        scaled_two * norm_gains[1].astype(jnp.float32) + shifts[1].astype(jnp.float32)
    ).astype(jnp.bfloat16)
    pre_act = jnp.dot(normed_two, fc1_weight, preferred_element_type=jnp.float32) + fc1_bias.astype(
        jnp.float32
    )
    activated = jax.nn.gelu(pre_act, approximate=False).astype(jnp.bfloat16)
    return (mixed, scaled_two, factor_two, normed_two, pre_act, activated)


def shards(
    tokens,
    clip_starts,
    cls_index,
    norm_gains,
    shifts,
    qkv_weight,
    qv_bias,
    out_weight,
    fc1_weight,
    fc1_bias,
    fc2_weight,
    cotangent,
):
    masks = jax.vmap(visible)(clip_starts, cls_index)
    front = front_part(tokens, masks, norm_gains, shifts, qkv_weight, qv_bias, out_weight)
    (
        inputs,
        scaled_one,
        factor_one,
        normed_one,
        queries,
        key_rows,
        value_rows,
        context,
        log_total,
        partial_value,
    ) = front
    attn_total = lax.psum(partial_value.astype(jnp.bfloat16), "tensor").astype(jnp.float32)
    middle = middle_part(inputs, attn_total, norm_gains, shifts, fc1_weight, fc1_bias)
    mixed, scaled_two, factor_two, normed_two, pre_act, activated = middle
    mlp_total = lax.psum(
        jnp.dot(activated, fc2_weight, preferred_element_type=jnp.float32).astype(jnp.bfloat16),
        "tensor",
    ).astype(jnp.float32)
    layer_out = (mixed + mlp_total + shifts[3].astype(jnp.float32)).astype(jnp.bfloat16)
    front = front_part(tokens, masks, norm_gains, shifts, qkv_weight, qv_bias, out_weight)
    (
        inputs,
        scaled_one,
        factor_one,
        normed_one,
        queries,
        key_rows,
        value_rows,
        context,
        log_total,
        partial_value,
    ) = front
    attn_again = lax.psum(partial_value.astype(jnp.bfloat16), "tensor").astype(jnp.float32)
    middle = middle_part(inputs, attn_again, norm_gains, shifts, fc1_weight, fc1_bias)
    mixed, scaled_two, factor_two, normed_two, pre_act, activated = middle
    total_rows = tokens.shape[0]
    share_rows = total_rows // lax.axis_size("tensor")
    row_offset = lax.axis_index("tensor") * share_rows

    def own_rows(array):
        return lax.dynamic_slice_in_dim(array, row_offset, share_rows, 0)

    grad_out = cotangent.astype(jnp.float32)
    fc2_grad = contract_rows(activated, cotangent)
    grad_act = contract_cols(cotangent, fc2_weight)
    gelu_back = jax.vjp(lambda value: jax.nn.gelu(value, approximate=False), pre_act)[1]
    grad_pre = gelu_back(grad_act)[0].astype(jnp.bfloat16)
    fc1_grad = contract_rows(normed_two, grad_pre)
    fc1_bias_grad = jnp.sum(grad_pre.astype(jnp.float32), axis=0)
    row_block = grad_pre
    grad_two = lax.psum_scatter(
        contract_cols(row_block, fc1_weight).astype(jnp.bfloat16),
        "tensor",
        scatter_dimension=0,
        tiled=True,
    ).astype(jnp.float32)
    scaled_two_own = own_rows(scaled_two)
    mid_own = own_rows(grad_out) + norm_back(
        grad_two, scaled_two_own, own_rows(factor_two), norm_gains[1].astype(jnp.float32)
    )
    mid_grad = lax.all_gather(mid_own.astype(jnp.bfloat16), "tensor", axis=0, tiled=True).astype(
        mid_own.dtype
    )
    mid_low = mid_grad.astype(jnp.bfloat16)
    out_grad = contract_rows(context, mid_low)
    grad_context = contract_cols(mid_low, out_weight).astype(jnp.bfloat16).reshape(queries.shape)
    grad_query, grad_key, grad_value = lax.map(
        attend_back, (queries, key_rows, value_rows, masks, log_total, grad_context)
    )
    local_width = context.shape[1]
    stacked = jnp.stack(
        [
            grad_query.reshape(total_rows, local_width),
            grad_key.reshape(total_rows, local_width),
            grad_value.reshape(total_rows, local_width),
        ],
        axis=1,
    )
    qkv_grad = jnp.einsum("td,tce->dce", normed_one, stacked, preferred_element_type=jnp.float32)
    qv_bias_grad = jnp.stack(
        [
            jnp.sum(stacked[:, 0].astype(jnp.float32), axis=0),
            jnp.sum(stacked[:, 2].astype(jnp.float32), axis=0),
        ]
    )
    qkv_grad, qv_bias_grad, out_grad, fc1_grad, fc1_bias_grad, fc2_grad = lax.psum(
        (qkv_grad, qv_bias_grad, out_grad, fc1_grad, fc1_bias_grad, fc2_grad), "dp"
    )
    row_block = stacked
    grad_one = lax.psum_scatter(
        jnp.einsum("tce,dce->td", row_block, qkv_weight, preferred_element_type=jnp.float32).astype(
            jnp.bfloat16
        ),
        "tensor",
        scatter_dimension=0,
        tiled=True,
    ).astype(jnp.float32)
    scaled_one_own = own_rows(scaled_one)
    input_own = mid_own + norm_back(
        grad_one, scaled_one_own, own_rows(factor_one), norm_gains[0].astype(jnp.float32)
    )
    input_grad = lax.all_gather(input_own.astype(jnp.bfloat16), "tensor", axis=0, tiled=True)
    gain_part = jnp.stack(
        [jnp.sum(grad_one * scaled_one_own, axis=0), jnp.sum(grad_two * scaled_two_own, axis=0)]
    )
    shift_part = jnp.stack(
        [
            jnp.sum(grad_one, axis=0),
            jnp.sum(grad_two, axis=0),
            jnp.sum(mid_own, axis=0),
            jnp.sum(own_rows(grad_out), axis=0),
        ]
    )
    gain_total, shift_total = lax.psum((gain_part, shift_part), ("dp", "tensor"))
    return (
        layer_out,
        input_grad,
        gain_total,
        shift_total,
        qkv_grad,
        qv_bias_grad,
        out_grad,
        fc1_grad,
        fc1_bias_grad,
        fc2_grad,
    )


def solution(mesh):
    return jax.shard_map(
        shards,
        mesh=mesh,
        in_specs=(
            P("dp", None),
            P("dp", None),
            P("dp", None),
            P(),
            P(),
            P(None, None, "tensor"),
            P(None, "tensor"),
            P("tensor", None),
            P(None, "tensor"),
            P("tensor"),
            P("tensor", None),
            P("dp", None),
        ),
        out_specs=(
            P("dp", None),
            P("dp", None),
            P(),
            P(),
            P(None, None, "tensor"),
            P(None, "tensor"),
            P("tensor", None),
            P(None, "tensor"),
            P("tensor"),
            P("tensor", None),
        ),
        check_vma=False,
    )
```

profile of v0, /device:TPU:8, one launch (start us, length us, event | category | flops | bytes accessed | tf_op | source)
XLA Modules:
  0.0 821.4 jit_solution(16355355827297663258)
XLA Ops:
  31.3 18.6 %while.37 = (s32[]{:T(128)}, bf16[2,896,3,64]{1,3,2,0:T(8,128)(2,1)}, f32[2,3,896]{2,1,0:T(4,128)S(1)}, bf16[2,896,3,64]{1,3,2,0:T(8,128)(2,1)}, pred[2,896,896]...) while((s32[]{:T(128)}, ...), condition=%wide.region_15.16_spmd, body=%wide.region_12.15_spmd.sunk | while | flops 645633408 | bytes 42655416 | solution.py:110
  50.8 53.4 %while.36 = (s32[]{:T(128)}, bf16[2,896,3,64]{1,3,2,0:T(8,128)(2,1)}, bf16[2,896,3,64]{1,3,2,0:T(8,128)(2,1)}, pred[2,896,896]{1,2,0:T(8,128)(4,1)S(1)}, bf16[2,...) while((s32[]{:T(128)}, bf16[2,896,3,64]{1,3,2,0:T(8,128)(2,1)}, ...), condition=%wide.region_7.8_spmd, body=%wide.region_4.7_spmd.sunk | while | flops 636003200 | bytes 50604716 | solution.py:110
  51.4 6.1 fusion.214
  57.6 14.7 %fusion.215 = (f32[3,896]{1,0:T(4,128)S(1)}, f32[3,896,896]{1,2,0:T(8,128)}) fusion(f32[3,896,896]{1,2,0:T(8,128)} %fusion.214, pred[896,896]{0,1:T(8,128)(4,1)S(1)} %dynamic-slice_bitcast_fusion.8), kind=kOutput, calls=%fused_computation.250.clone.1 | output fusion | flops 14451583 | bytes 20081152 | tf_op jit(solution)/shard_map/while/body/eval_jaxpr/sub | solution.py:55
  72.2 4.6 fusion.216
  77.8 6.1 fusion.214
  84.0 14.7 %fusion.215 = (f32[3,896]{1,0:T(4,128)S(1)}, f32[3,896,896]{1,2,0:T(8,128)}) fusion(f32[3,896,896]{1,2,0:T(8,128)} %fusion.214, pred[896,896]{0,1:T(8,128)(4,1)S(1)} %dynamic-slice_bitcast_fusion.8), kind=kOutput, calls=%fused_computation.250.clone.1 | output fusion | flops 14451583 | bytes 20081152 | tf_op jit(solution)/shard_map/while/body/eval_jaxpr/sub | solution.py:55
  98.6 4.6 fusion.216
  113.1 108.2 %all-reduce.12.cloned.1.call-done = (bf16[1792,768]{1,0:T(8,128)(2,1)}, bf16[1792,768]{1,0:T(8,128)(2,1)}) async-done(((bf16[1792,768]{1,0:T(8,128)(2,1)}, bf16[1792,768]{1,0:T(8,128)(2,1)}), (bf16[1792,768]{1,0:T(8,128)(2,1)}, bf16[1792,768]{1,0:T(8,128)(2,1)})) %all-reduce.12.cloned.1.call-update) | async-done | bytes 5505040 | tf_op jit(solution)/shard_map/psum | solution.py:168
  221.3 5.8 fusion.95
  227.2 5.5 multiply_reduce_fusion.1
  232.7 19.6 %convolution_convert_fusion.2 = bf16[1792,768]{1,0:T(8,128)(2,1)} fusion(bf16[768,768]{1,0:T(8,128)(2,1)S(1)} %copy-done, bf16[768,768]{1,0:T(8,128)(2,1)} %param.26, bf16[1792,768]{1,0:T(8,128)(2,1)} %get-tuple-element.283, bf16[1792,768]{1,0:T(8,128)(2,1)} %param.18, f32[768]{0:T(1024)S(1)} %convert_element_type.179, f32[768]{0:T(1024)S(1)} %copy-done.37, ...), kind=kOutput, calls=%fused_computation.143 | convolution fusion | flops 4332453888 | bytes 10643456 | tf_op jit(solution)/shard_map/dot_general | solution.py:172
  252.4 62.3 %all-reduce.8.cloned.1.call-done = bf16[1792,768]{1,0:T(8,128)(2,1)} async-done(((bf16[1792,768]{1,0:T(8,128)(2,1)}), bf16[1792,768]{1,0:T(8,128)(2,1)}) %all-reduce.8.cloned.1.call-update) | async-done | bytes 2752528 | tf_op jit(solution)/shard_map/psum | solution.py:171
  314.7 6.8 subtract_multiply_fusion
  325.3 16.4 %convert_reduce_fusion.1 = (f32[768]{0:T(1024)}, bf16[1792,768]{1,0:T(8,128)(2,1)S(1)}, f32[1792,768]{1,0:T(8,128)}) fusion(f32[1792,768]{1,0:T(8,128)S(1)} %fusion.126, f32[768]{0:T(1024)S(1)} %convert_element_type.179, bf16[1792,768]{1,0:T(8,128)(2,1)S(1)} %copy-done.41, bf16[768,768]{1,0:T(8,128)(2,1)S(1)} %copy-done), kind=kOutput, calls=%fused_computation.102 | convolution fusion | flops 2217147648 | bytes 17700864 | tf_op jit(solution)/shard_map/dot_general | solution.py:39
  343.2 3.9 convolution_convert_fusion
  347.2 35.6 %reduce-scatter.3.cloned.1.call-done = bf16[448,768]{1,0:T(8,128)(2,1)} async-done(((bf16[1792,768]{1,0:T(8,128)(2,1)}), bf16[448,768]{1,0:T(8,128)(2,1)}) %reduce-scatter.3.cloned.1.call-update) | async-done | bytes 688144 | tf_op jit(solution)/shard_map/reduce_scatter | solution.py:207
  389.8 26.4 %all-gather.3.cloned.1.call-done = bf16[1792,768]{1,0:T(8,128)(2,1)} async-done(((bf16[448,768]{1,0:T(8,128)(2,1)}), bf16[1792,768]{1,0:T(8,128)(2,1)}) %all-gather.3.cloned.1.call-update) | async-done | bytes 2752528 | tf_op jit(solution)/shard_map/all_gather | solution.py:217
  427.6 58.1 %while.38 = (s32[]{:T(128)}, bf16[2,896,3,64]{1,3,2,0:T(8,128)(2,1)}, bf16[2,896,3,64]{1,3,2,0:T(8,128)(2,1)}, bf16[2,896,3,64]{1,3,2,0:T(8,128)(2,1)}, bf16[2,8...) while((s32[]{:T(128)}, ...), condition=%wide.region_24.25_spmd, body=%wide.region_22.24_spmd.sunk | while | flops 1566348672 | bytes 146978096 | solution.py:223
  430.3 6.7 multiply_reduce_fusion.4
  437.0 9.7 %multiply_convert_fusion.4 = bf16[3,896,896]{1,2,0:T(8,128)(2,1)} fusion(f32[3,896,896]{1,2,0:T(8,128)} %get-tuple-element.455, f32[3,896,896]{1,2,0:T(8,128)} %copy-done.3, f32[3,896]{1,0:T(4,128)S(1)} %get-tuple-element.456), kind=kLoop, calls=%fused_computation.46.clone.1 | loop fusion | flops 7225344 | bytes 24095232 | tf_op jit(solution)/shard_map/while/body/eval_jaxpr/convert_element_type | solution.py:81
  446.7 6.3 fusion.232
  459.1 6.7 multiply_reduce_fusion.4
  465.8 9.7 %multiply_convert_fusion.4 = bf16[3,896,896]{1,2,0:T(8,128)(2,1)} fusion(f32[3,896,896]{1,2,0:T(8,128)} %get-tuple-element.455, f32[3,896,896]{1,2,0:T(8,128)} %copy-done.3, f32[3,896]{1,0:T(4,128)S(1)} %get-tuple-element.456), kind=kLoop, calls=%fused_computation.46.clone.1 | loop fusion | flops 7225344 | bytes 24095232 | tf_op jit(solution)/shard_map/while/body/eval_jaxpr/convert_element_type | solution.py:81
  475.5 6.3 fusion.232
  492.9 5.1 bitcast_convert_fusion
  498.1 35.5 %reduce-scatter.5.cloned.1.call-done = bf16[448,768]{1,0:T(8,128)(2,1)} async-done(((bf16[1792,768]{1,0:T(8,128)(2,1)}), bf16[448,768]{1,0:T(8,128)(2,1)}) %reduce-scatter.5.cloned.1.call-update) | async-done | bytes 688144 | tf_op jit(solution)/shard_map/reduce_scatter | solution.py:246
  538.8 7.3 fusion.125
  546.1 8.7 %fusion.97 = f32[768,768]{1,0:T(8,128)} fusion(bf16[1792,768]{1,0:T(8,128)(2,1)S(1)} %copy-done.42, f32[1792,768]{1,0:T(8,128)} %get-tuple-element.287, f32[1792,768]{1,0:T(8,128)} %copy-done.67, f32[768]{0:T(1024)S(1)} %convert_element_type.179), kind=kOutput, calls=%fused_computation.145 | convolution fusion | flops 2119434240 | bytes 16124928 | tf_op jit(solution)/shard_map/dot_general | solution.py:33
  561.3 19.7 %all-reduce.1 = (f32[2,192]{1,0:T(2,128)}, f32[768]{0:T(1024)}) all-reduce(f32[2,192]{1,0:T(2,128)S(1)} %pad_maximum_fusion.2, f32[768]{0:T(1024)S(1)} %copy-done.57), channel_id=1, replica_groups=mesh['dp'=8,'tensor'=4] {'dp'}, use_global_device_ids=true, to_apply=%region_39.40 | all-reduce | flops 1152 | bytes 9216 | tf_op jit(solution)/shard_map/psum | solution.py:242
  581.0 44.9 %all-reduce = (f32[2,768]{1,0:T(2,128)}, f32[4,768]{1,0:T(4,128)}) all-reduce(f32[2,768]{1,0:T(2,128)S(1)} %pad_maximum_fusion.1, f32[4,768]{1,0:T(4,128)S(1)} %pad_maximum_fusion), channel_id=1, replica_groups=mesh['dp'=8,'tensor'=4] {'dp','tensor'}, use_global_device_ids=true, to_apply=%region_30.31 | all-reduce | flops 4608 | bytes 36864 | tf_op jit(solution)/shard_map/psum | solution.py:270
  625.9 179.9 %all-reduce.10.cloned.1.call-done = (f32[768,3,192]{0,2,1:T(8,128)}, f32[192,768]{1,0:T(8,128)}, f32[768,768]{1,0:T(8,128)}, f32[768,768]{1,0:T(8,128)}) async-done(((f32[768,3,192]{0,2,1:T(8,128)}, f32[192,768]{1,0:T(8,128)}, f32[768,768]{1,0:T(8,128)}, f32[768,768]{1,0:T(8,128)}), (f32[768,3,192]{0,2,1:T(8,128)}, f32[192,768]{1,0:T(8,128)}, f32[768,768]{1,0:T(8,128)}, ...) | async-done | bytes 7077904 | tf_op jit(solution)/shard_map/psum | solution.py:242
  (280 shorter events, 117.2 us)
Async XLA Ops:
  7.2 225.5 %copy-start = (bf16[768,768]{1,0:T(8,128)(2,1)S(1)}, bf16[768,768]{1,0:T(8,128)(2,1)}, u32[]{:S(2)}) copy-start(bf16[768,768]{1,0:T(8,128)(2,1)} %param.28) | copy-start | bytes 3538948
  7.2 214.1 %all-reduce.12.cloned.1.call-start = ((), (), s32[]{:S(2)}) async-start(), calls=%async_computation.8 | async-start | bytes 11010048 | tf_op jit(solution)/shard_map/psum | solution.py:168
  57.6 14.7 %copy-start.14 = (bf16[2,896,3,64]{1,3,2,0:T(8,128)(2,1)S(1)}, bf16[2,896,3,64]{1,3,2,0:T(8,128)(2,1)}, u32[]{:S(2)}) copy-start(bf16[2,896,3,64]{1,3,2,0:T(8,128)(2,1)} %get-tuple-element.473) | copy-start | bytes 2064388 | tf_op jit(solution)/shard_map/while
  57.6 14.7 %copy-start.26 = (bf16[2,896,3,64]{1,3,2,0:T(8,128)(2,1)S(1)}, bf16[2,896,3,64]{1,3,2,0:T(8,128)(2,1)}, u32[]{:S(2)}) copy-start(bf16[2,896,3,64]{1,3,2,0:T(8,128)(2,1)} %get-tuple-element.465) | copy-start | bytes 2064388 | tf_op jit(solution)/shard_map/while
  84.0 14.7 %copy-start.14 = (bf16[2,896,3,64]{1,3,2,0:T(8,128)(2,1)S(1)}, bf16[2,896,3,64]{1,3,2,0:T(8,128)(2,1)}, u32[]{:S(2)}) copy-start(bf16[2,896,3,64]{1,3,2,0:T(8,128)(2,1)} %get-tuple-element.473) | copy-start | bytes 2064388 | tf_op jit(solution)/shard_map/while
  84.0 14.7 %copy-start.26 = (bf16[2,896,3,64]{1,3,2,0:T(8,128)(2,1)S(1)}, bf16[2,896,3,64]{1,3,2,0:T(8,128)(2,1)}, u32[]{:S(2)}) copy-start(bf16[2,896,3,64]{1,3,2,0:T(8,128)(2,1)} %get-tuple-element.465) | copy-start | bytes 2064388 | tf_op jit(solution)/shard_map/while
  110.5 110.8 %copy-start.46 = (f32[768]{0:T(1024)S(1)}, f32[768]{0:T(1024)}, u32[]{:S(2)}) copy-start(f32[768]{0:T(1024)} %get-tuple-element.222) | copy-start | bytes 9220
  113.0 114.1 %copy-start.44 = (f32[1792]{0:T(1024)S(1)}, f32[1792]{0:T(1024)}, u32[]{:S(2)}) copy-start(f32[1792]{0:T(1024)} %copy-done.43) | copy-start | bytes 21508
  113.0 114.1 %copy-start.48 = (f32[1792]{0:T(1024)S(1)}, f32[1792]{0:T(1024)}, u32[]{:S(2)}) copy-start(f32[1792]{0:T(1024)} %copy-done.47) | copy-start | bytes 21508
  113.0 201.7 %all-reduce.8.cloned.1.call-start = ((), (), s32[]{:S(2)}) async-start(), calls=%async_computation.2 | async-start | bytes 5505024 | tf_op jit(solution)/shard_map/psum | solution.py:171
  232.7 82.0 %copy-start.55 = (f32[768]{0:T(1024)S(1)}, f32[768]{0:T(1024)}, u32[]{:S(2)}) copy-start(f32[768]{0:T(1024)} %get-tuple-element.221) | copy-start | bytes 9220
  252.3 130.5 %reduce-scatter.3.cloned.1.call-start = ((), (), s32[]{:S(2)}) async-start(), calls=%async_computation.3 | async-start | bytes 3440640 | tf_op jit(solution)/shard_map/reduce_scatter | solution.py:207
  325.3 16.4 %copy-start.67 = (f32[1792,768]{1,0:T(8,128)}, f32[1792,768]{1,0:T(8,128)S(1)}, u32[]{:S(2)}) copy-start(f32[1792,768]{1,0:T(8,128)S(1)} %fusion.126) | copy-start | bytes 16515076
  347.1 69.1 %copy-start.32 = (bf16[192,768]{1,0:T(8,128)(2,1)S(1)}, bf16[192,768]{1,0:T(8,128)(2,1)}, u32[]{:S(2)}) copy-start(bf16[192,768]{1,0:T(8,128)(2,1)} %param.25) | copy-start | bytes 884740
  347.1 69.1 %all-gather.3.cloned.1.call-start = ((), (), s32[]{:S(2)}) async-start(), calls=%async_computation.4 | async-start | bytes 3440640 | tf_op jit(solution)/shard_map/all_gather | solution.py:217
  389.8 37.8 %copy-start.7 = (bf16[2,896,3,64]{1,3,2,0:T(8,128)(2,1)S(1)}, bf16[2,896,3,64]{1,3,2,0:T(8,128)(2,1)}, u32[]{:S(2)}) copy-start(bf16[2,896,3,64]{1,3,2,0:T(8,128)(2,1)} %get-tuple-element.577) | copy-start | bytes 2064388
  389.8 37.8 %copy-start.40 = (f32[2,3,896]{2,1,0:T(4,128)S(1)}, f32[2,3,896]{2,1,0:T(4,128)}, u32[]{:S(2)}) copy-start(f32[2,3,896]{2,1,0:T(4,128)} %copy-done.39) | copy-start | bytes 64516
  389.8 143.8 %reduce-scatter.5.cloned.1.call-start = ((), (), s32[]{:S(2)}) async-start(), calls=%async_computation.5 | async-start | bytes 3440640 | tf_op jit(solution)/shard_map/reduce_scatter | solution.py:246
  446.7 8.0 copy-start.16
  475.5 7.9 copy-start.16
  492.9 40.7 %copy-start.51 = (f32[768]{0:T(1024)S(1)}, f32[768]{0:T(1024)}, u32[]{:S(2)}) copy-start(f32[768]{0:T(1024)} %copy-done.50) | copy-start | bytes 9220
  498.0 37.7 %copy-start.12 = (f32[448,768]{1,0:T(8,128)S(1)}, f32[448,768]{1,0:T(8,128)}, u32[]{:S(2)}) copy-start(f32[448,768]{1,0:T(8,128)} %copy-done.11) | copy-start | bytes 4128772
  498.0 40.8 %copy-start.38 = (f32[768]{0:T(1024)S(1)}, f32[768]{0:T(1024)}, u32[]{:S(2)}) copy-start(f32[768]{0:T(1024)} %get-tuple-element.224) | copy-start | bytes 9220
  498.0 127.9 %all-gather.5.cloned.1.call-start = ((), (), s32[]{:S(2)}) async-start(), calls=%async_computation.6 | async-start | bytes 3440640 | tf_op jit(solution)/shard_map/all_gather | solution.py:258
  538.5 267.3 %all-reduce.10.cloned.1.call-start = ((), (), s32[]{:S(2)}) async-start(), calls=%async_computation.7 | async-start | bytes 14155776 | tf_op jit(solution)/shard_map/psum | solution.py:242
  538.7 7.3 copy-start.42
  546.1 8.7 %copy-start.20 = (bf16[24,8,2,896]{3,1,2,0:T(8,128)(2,1)S(1)}, bf16[24,8,2,896]{3,1,2,0:T(8,128)(2,1)}, u32[]{:S(2)}) copy-start(bf16[24,8,2,896]{3,1,2,0:T(8,128)(2,1)} %copy-done.19) | copy-start | bytes 2064388
  546.1 8.7 %copy-start.64 = (bf16[1792,768]{1,0:T(8,128)(2,1)S(1)}, bf16[1792,768]{1,0:T(8,128)(2,1)}, u32[]{:S(2)}) copy-start(bf16[1792,768]{1,0:T(8,128)(2,1)} %all-gather.3.cloned.1.call-done) | copy-start | bytes 8257540
  546.1 10.2 %copy-start.6 = (bf16[1792,768]{1,0:T(8,128)(2,1)S(1)}, bf16[1792,768]{1,0:T(8,128)(2,1)}, u32[]{:S(2)}) copy-start(bf16[1792,768]{1,0:T(8,128)(2,1)} %param.18) | copy-start | bytes 8257540
  546.1 10.2 %copy-start.36 = (bf16[1792,3,192]{0,2,1:T(8,128)(2,1)S(1)}, bf16[1792,3,192]{0,2,1:T(8,128)(2,1)}, u32[]{:S(2)}) copy-start(bf16[1792,3,192]{0,2,1:T(8,128)(2,1)} %copy-done.35) | copy-start | bytes 6193156
  546.1 10.2 %copy-start.45 = (f32[1792]{0:T(1024)S(1)}, f32[1792]{0:T(1024)}, u32[]{:S(2)}) copy-start(f32[1792]{0:T(1024)} %copy-done.43) | copy-start | bytes 21508
  546.1 10.2 %copy-start.59 = (f32[768]{0:T(1024)S(1)}, f32[768]{0:T(1024)}, u32[]{:S(2)}) copy-start(f32[768]{0:T(1024)} %copy-done.58) | copy-start | bytes 9220
  (55 other events, 185.4 us)
Sparse Core Ops, SparseCore 0:
  113.1 108.1 all-reduce.11
  252.5 62.1 all-reduce.7
  347.2 35.5 reduce-scatter.2
  389.9 26.2 all-gather.2
  498.1 35.4 reduce-scatter.4
  538.6 26.2 all-gather.4
  570.5 235.2 all-reduce.9
where the time goes:
time: 829 us; the launch traced here: 821 us
  waiting for transfers between devices  448 us (54%)
  matrix products  149 us (18%)
  other arithmetic  93.2 us (11%)
  blocking collectives  64.6 us (8%)
  local copies, waits for them, and re-layouts  50 us (6%)
  between operations  15 us (2%)
    psum x1, waiting for transfers between devices, shards(): lax.psum((qkv_grad, qv_bias_grad, out_grad, fc1_grad, fc1_bias_grad, fc2_...  180 us
    psum x1, waiting for transfers between devices, shards(): lax.psum(partial_value.astype(jnp.bfloat16), 'tensor').astype(jnp.float32)  108 us
    psum x1, waiting for transfers between devices, shards(): lax.psum(jnp.dot(activated, fc2_weight, preferred_element_type=jnp.float3...  62.3 us
    psum x1, blocking collectives, shards(): lax.psum((gain_part, shift_part), ('dp', 'tensor'))  44.9 us
    reduce_scatter x1, waiting for transfers between devices, shards(): lax.psum_scatter(contract_cols(row_block, fc1_weight).astype(jnp.bfloat16...  35.6 us
    reduce_scatter x1, waiting for transfers between devices, shards(): lax.psum_scatter(jnp.einsum('tce,dce->td', row_block, qkv_weight, preferr...  35.5 us
    dot_general x6, matrix products, raw_scores(): jnp.einsum('qhd,khd->hqk', queries, key_rows, preferred_element_type=jnp....  31.9 us
    sub x2, other arithmetic, attend(): exponent = jnp.exp(scores - row_max)  29.3 us
  transfers between devices with their start and end apart: 7, of which 6 were waited for; matrix products, arithmetic and copies ran while one was open for 3% of the time, Pallas kernels for 0%

commit v1 on v0

v1 whole, which is shorter than its diff:
```python
import functools

import jax
import jax.numpy as jnp
from jax import lax
from jax.experimental import pallas as pl
from jax.experimental.pallas import tpu as pltpu
from jax.sharding import PartitionSpec as P

HEAD = 64
EPS = 1e-06
F32 = jnp.float32
BF16 = jnp.bfloat16
BLOCK = 112
CHUNKS = 2
MESH = pl.DeviceIdType.MESH


def nn(a, b):
    return lax.dot_general(a, b, (((1,), (0,)), ((), ())), preferred_element_type=F32)


def nt(a, b):
    return lax.dot_general(a, b, (((1,), (1,)), ((), ())), preferred_element_type=F32)


def tn(a, b):
    return lax.dot_general(a, b, (((0,), (0,)), ((), ())), preferred_element_type=F32)


def normalize(x):
    centre = x - jnp.mean(x, axis=-1, keepdims=True)
    factor = lax.rsqrt(jnp.mean(centre * centre, axis=-1, keepdims=True) + EPS)
    return centre * factor, factor


def norm_back(grad, scaled, factor, gain):
    inner = grad * gain
    return factor * (
        inner
        - jnp.mean(inner, axis=-1, keepdims=True)
        - scaled * jnp.mean(inner * scaled, axis=-1, keepdims=True)
    )


def column_sum(x):
    return jnp.sum(x, axis=0, keepdims=True)


def loop(n, body):
    lax.fori_loop(0, n, lambda i, carry: (body(i), carry)[1], 0)


def rows_at(i, size, base=0):
    return pl.ds(pl.multiple_of(base + i * size, 16), size)


def remote(src, dst, send_sem, recv_sem, axis, index):
    return pltpu.make_async_remote_copy(
        src_ref=src, dst_ref=dst, send_sem=send_sem, recv_sem=recv_sem,
        device_id={axis: index}, device_id_type=MESH,
    )


class Pair:
    def __init__(self, send, mine, from_core, from_chip, sems, core, chip):
        self.send, self.mine, self.from_core, self.from_chip = send, mine, from_core, from_chip
        self.to_core = remote(send, from_core, sems.at[0], sems.at[1], "tensor", core)
        self.to_chip = remote(mine, from_chip, sems.at[2], sems.at[3], "tensor", chip)

    def start(self):
        self.to_core.start()

    def gather(self):
        self.to_core.wait()

        def body(i):
            r = rows_at(i, BLOCK)
            self.mine[r, :] = (self.mine[r, :].astype(F32) + self.from_core[r, :].astype(F32)).astype(BF16)

        loop(self.mine.shape[0] // BLOCK, body)

    def middle(self):
        self.gather()
        self.to_chip.start()

    def finish(self):
        self.to_chip.wait()

    def total(self, r):
        return self.mine[r, :].astype(F32) + self.from_chip[r, :].astype(F32)


def layer_kernel(
    seqs, length, heads, n_dp, group, extra,
    st_ref, mk_ref, gain_ref, shift_ref, qvb_ref, b1_ref, tok_h, cot_h, w_h, ow_h, fc1_h, fc2_h,
    out_h, grad_h, gmat_h, small_ref, e_h,
    tok, cot, w_ref, ow_ref, fc1, fc2, h1_ref, qa, ka, va, es, st_s, ct_s, ctxt_ref, linv_ref,
    send, mine, fcore, fchip, x1_ref, dx_ref, h2_ref, dxs, dxr_mine, dxr_other, ds_s, da_s, dcx_s, dq_s,
    dk_s, dv_s, gbuf, rx, rz, re, sv, svr,
    load_sem, e_sem, pair_sem, h2_sem, dx_sem, red_sem, out_sem, small_sem,
):
    half = length // 2
    width = tok.shape[1]
    hidden = fc1.shape[1]
    local = heads * HEAD
    clips = st_ref.shape[1]
    t = lax.axis_index("tensor")
    dp = lax.axis_index("dp")
    c = t % 2
    core = t + 1 - 2 * c
    chip = (t + 2) % 4
    own = pl.multiple_of(c * half, half)
    other = pl.multiple_of((1 - c) * half, half)
    xi = dp % 2
    xpeer = dp + 1 - 2 * xi
    zi = (dp // 2) % group
    zpeers = [dp + 2 * ((zi + k) % group - zi) for k in range(1, group)]
    ebits = [2 * group * 2**k for k in range(extra)]
    epeers = [dp + bit - 2 * bit * ((dp // bit) % 2) for bit in ebits]

    def load(k, src, dst):
        cp = pltpu.make_async_copy(src, dst, load_sem.at[k])
        cp.start()
        return cp

    tok_rows = [pl.ds(s * length, length) for s in range(seqs)]
    load_tok0 = load(0, tok_h.at[tok_rows[0]], tok.at[tok_rows[0]])
    load_w = load(1, w_h, w_ref)
    load_tok1 = load(2, tok_h.at[pl.ds(length, (seqs - 1) * length)], tok.at[pl.ds(length, (seqs - 1) * length)])
    load_ow = load(3, ow_h, ow_ref)
    load_fc1 = load(4, fc1_h, fc1)
    load_cot = load(5, cot_h, cot)
    load_fc2 = load(6, fc2_h, fc2)

    barrier = pltpu.get_barrier_semaphore()
    for peer in (core, chip):
        pl.semaphore_signal(barrier, inc=1, device_id={"tensor": peer}, device_id_type=MESH)
    for peer in [xpeer] + zpeers + epeers:
        pl.semaphore_signal(barrier, inc=1, device_id={"dp": peer}, device_id_type=MESH)
    pl.semaphore_wait(barrier, 3 + len(zpeers) + len(epeers))

    def pair(b, q):
        return Pair(send.at[b], mine.at[q], fcore.at[b], fchip.at[q], pair_sem.at[q], core, chip)

    pair_a = [pair(s, s) for s in range(seqs)]
    pair_d = [pair(seqs + s, seqs + s) for s in range(seqs)]
    pair_m = [pair(2 * seqs, 2 * seqs + s) for s in range(seqs)]
    pair_g = [
        Pair(send.at[s], mine.at[s], fcore.at[s], fchip.at[s], pair_sem.at[3 * seqs + s], core, chip)
        for s in range(seqs)
    ]

    sv[...] = jnp.zeros_like(sv)

    def add_sum(row, value):
        sv[row : row + 1, : value.shape[1]] += value

    def spill(j, slot):
        return pltpu.make_async_copy(es.at[slot], e_h.at[j], e_sem.at[slot])

    def fetch(j, slot):
        return pltpu.make_async_copy(e_h.at[j], es.at[slot], e_sem.at[2 + slot])

    def project(s):
        gain = gain_ref[0:1, :].astype(F32)
        shift = shift_ref[0:1, :].astype(F32)
        qvb = qvb_ref[...].astype(F32)
        size = 128

        def body(i):
            r = rows_at(i, size)
            x = tok[rows_at(i, size, s * length), :].astype(F32)
            scaled, _ = normalize(x)
            h1 = (scaled * gain + shift).astype(BF16)
            h1_ref[s, r, :] = h1
            q = (nn(h1, w_ref[0]) + qvb[0:1]).astype(BF16).astype(F32) * 0.125
            q = q.astype(BF16)
            k = nn(h1, w_ref[1]).astype(BF16)
            v = (nn(h1, w_ref[2]) + qvb[1:2]).astype(BF16)
            pos = lax.broadcasted_iota(jnp.int32, (size, HEAD), 0) + i * size
            lane = lax.broadcasted_iota(jnp.int32, (size, HEAD), 1)
            clip = jnp.zeros((size, HEAD), jnp.int32) - 1
            mark = jnp.zeros((size, HEAD), jnp.int32)
            for n in range(clips):
                clip = clip + jnp.where(pos >= st_ref[s, n], 1, 0)
                mark = mark + jnp.where(pos == mk_ref[s, n], 1, 0)
            qf = jnp.where(lane == clip, 1.0, 0.0).astype(BF16)
            hide = (lane < clips) & (lane != clip) & (mark == 0)
            kf = jnp.where(hide, -1e30, 0.0).astype(BF16)
            vf = jnp.where(lane < 2, 1.0, 0.0).astype(BF16)
            for h in range(heads):
                cols = slice(h * HEAD, h * HEAD + HEAD)
                qa[s, h, r, :] = jnp.concatenate([q[:, cols], qf], axis=1)
                ka[s, h, r, :] = jnp.concatenate([k[:, cols], kf], axis=1)
                va[s, h, r, :] = jnp.concatenate([v[:, cols], vf], axis=1)

        loop(length // size, body)

    spans = [(t0, min(256, length - t0)) for t0 in range(0, length, 256)]

    def attend(s):
        def head(h):
            j = s * heads + h
            slot = lax.rem(j, 2)

            @pl.when(j >= 2)
            def _():
                spill(j, slot).wait()

            v = va[s, h, :, :HEAD]
            for i, (t0, n) in enumerate(spans):
                sl = i % 2
                st_s[sl, :, :n] = nt(ka[s, h], qa[s, h, t0 : t0 + n])
                ch = 64
                m = None
                for u in range(0, length, ch):
                    x = jnp.max(st_s[sl, u : u + ch, :n].reshape(ch // 8, 8, n), axis=0)
                    m = x if m is None else jnp.maximum(m, x)
                m = jnp.max(m, axis=0, keepdims=True)
                tot = None
                for u in range(0, length, ch):
                    x = jnp.exp(st_s[sl, u : u + ch, :n] - m)
                    es[slot, u : u + ch, t0 : t0 + n] = x.astype(BF16)
                    x = jnp.sum(x.reshape(ch // 8, 8, n), axis=0)
                    tot = x if tot is None else tot + x
                inv = 1.0 / jnp.sum(tot, axis=0, keepdims=True)
                linv_ref[s, h, :, t0 : t0 + n] = jnp.broadcast_to(inv, (8, n))
                ct_s[rows_at(h, HEAD), t0 : t0 + n] = tn(v, es[slot, :, t0 : t0 + n]) * inv
            spill(j, slot).start()

        loop(heads, head)
        ctxt_ref[s] = ct_s[...].astype(BF16)
        dq_s[0] = jnp.transpose(ct_s[...]).astype(BF16)

        def rows_out(dst, base):
            def body(i):
                dst[rows_at(i, BLOCK), :] = nn(dq_s[0, rows_at(i, BLOCK, base), :], ow_ref[...]).astype(BF16)

            loop(half // BLOCK, body)

        rows_out(send.at[s], other)
        pair_a[s].start()
        rows_out(mine.at[s], own)

    h2_copies = [
        remote(
            h2_ref.at[s, pl.ds(own, half)], h2_ref.at[s, pl.ds(own, half)], h2_sem.at[s, 0], h2_sem.at[s, 1],
            "tensor", core,
        )
        for s in range(seqs)
    ]

    def norm_two(s):
        pair_a[s].finish()
        g = gain_ref[1:2, :].astype(F32)
        b1 = shift_ref[1:2, :].astype(F32)
        b2 = shift_ref[2:3, :].astype(F32)

        def body(i):
            r = rows_at(i, BLOCK)
            x = tok[rows_at(i, BLOCK, s * length + own), :].astype(F32)
            x1 = x + pair_a[s].total(r) + b2
            x1_ref[s, r, :] = x1
            scaled, _ = normalize(x1)
            h2_ref[s, rows_at(i, BLOCK, own), :] = (scaled * g + b1).astype(BF16)

        loop(half // BLOCK, body)
        h2_copies[s].start()

    act_ref, dpre_ref = ds_s, dxs

    def feed_forward(s, base, mlp_dst, dh2_dst):
        size = BLOCK

        def body(i):
            r = rows_at(i, size, base)
            pre = nn(h2_ref[s, r, :], fc1[...]) + b1_ref[...].astype(F32)
            phi = 0.5 * (1.0 + lax.erf(pre * 0.7071067811865476))
            act = (pre * phi).astype(BF16)
            act_ref[r, :hidden] = act
            slope = phi + pre * (0.3989422804014327 * jnp.exp(-0.5 * pre * pre))
            dact = nt(cot[rows_at(i, size, s * length + base), :], fc2[...])
            dpre = (dact * slope).astype(BF16)
            dpre_ref[r, :hidden] = dpre
            add_sum(6, column_sum(dpre.astype(F32)))
            dh2_dst[rows_at(i, size), :] = nt(dpre, fc1[...]).astype(BF16)
            mlp_dst[rows_at(i, size), :] = nn(act, fc2[...]).astype(BF16)

        loop(half // size, body)

    def fc_grad(m, left, right, s, tile):
        def body(i):
            r = pl.ds(pl.multiple_of(i * tile, tile), tile)
            p = tn(left(r), right())
            if s > 0:
                p = p + gbuf[m, r, :].astype(F32)
            gbuf[m, r, :] = p.astype(BF16)

        loop(width // tile, body)

    def fc2_grad(s):
        fc_grad(0, lambda r: act_ref[:, r], lambda: cot[tok_rows[s], :], s, 256)

    def fc1_grad(s):
        fc_grad(1, lambda r: h2_ref[s, :, r], lambda: dpre_ref[:, :hidden], s, 256)

    piece = gbuf.shape[1] // CHUNKS // 2 // group

    def reduce_job(m, ch):
        job = m * CHUNKS + ch
        base = ch * (gbuf.shape[1] // CHUNKS)
        part = group * piece
        sem = iter(range(red_sem.shape[1]))
        two = lambda: (red_sem.at[job, next(sem)], red_sem.at[job, next(sem)])
        rows = lambda start, n: gbuf.at[m, pl.ds(pl.multiple_of(start, 16), n)]

        def add(start, n, sources):
            size = piece

            def body(i):
                r = rows_at(i, size, start)
                total = gbuf[m, r, :].astype(F32)
                for src in sources:
                    total = total + src[rows_at(i, size), :].astype(F32)
                gbuf[m, r, :] = total.astype(BF16)

            loop(n // size, body)

        mine_at = base + xi * part
        cp = remote(rows(base + (1 - xi) * part, part), rx.at[job], *two(), "dp", xpeer)
        cp.start()
        yield
        cp.wait()
        add(mine_at, part, [rx.at[job]])
        cps = [
            remote(rows(mine_at + ((zi + k + 1) % group) * piece, piece), rz.at[job, k], *two(), "dp", p)
            for k, p in enumerate(zpeers)
        ]
        for cp in cps:
            cp.start()
        yield
        for cp in cps:
            cp.wait()
        piece_at = mine_at + zi * piece
        add(piece_at, piece, [rz.at[job, k] for k in range(group - 1)])
        for k, p in enumerate(epeers):
            cp = remote(rows(piece_at, piece), re.at[job, k], *two(), "dp", p)
            cp.start()
            yield
            cp.wait()
            add(piece_at, piece, [re.at[job, k]])
        done = lambda start, n: gmat_h.at[m, pl.ds(pl.multiple_of(start, 16), n)]
        cps = [remote(rows(piece_at, piece), done(piece_at, piece), *two(), "dp", p) for p in zpeers]
        cps.append(pltpu.make_async_copy(rows(piece_at, piece), done(piece_at, piece), red_sem.at[job, next(sem)]))
        for cp in cps:
            cp.start()
        yield
        for cp in cps:
            cp.wait()
        cp = remote(done(mine_at, part), done(mine_at, part), *two(), "dp", xpeer)
        cp.start()
        yield
        cp.wait()

    def advance(*jobs):
        for job in jobs:
            next(job, None)

    def drain(*jobs):
        live = list(jobs)
        while live:
            live = [job for job in live if next(job, live) is not live]

    dx_copies = [
        remote(dxr_mine.at[s], dxr_other.at[s], dx_sem.at[s, 0], dx_sem.at[s, 1], "tensor", core)
        for s in range(seqs)
    ]

    def mid(s):
        pair_d[s].finish()
        g = gain_ref[1:2, :].astype(F32)

        def body(i):
            r = rows_at(i, BLOCK)
            dh2 = pair_d[s].total(r)
            scaled, factor = normalize(x1_ref[s, r, :])
            dy = cot[rows_at(i, BLOCK, s * length + own), :].astype(F32)
            dx = dy + norm_back(dh2, scaled, factor, g)
            dx_ref[s, r, :] = dx
            dxr_mine[s, r, :] = dx.astype(BF16)
            add_sum(1, column_sum(dh2 * scaled))
            add_sum(3, column_sum(dh2))
            add_sum(4, column_sum(dx))
            add_sum(5, column_sum(dy))

        loop(half // BLOCK, body)
        dx_copies[s].start()

    def back_setup(s):
        dxs[pl.ds(own, half), :] = dxr_mine[s]
        dx_copies[s].wait()
        dxs[pl.ds(other, half), :] = dxr_other[s]
        ct_s[...] = nt(ow_ref[...], dxs[...])
        for h in range(heads):
            lo = h * HEAD
            inv = linv_ref[s, h, 0:1, :]
            part = ct_s[lo : lo + HEAD, :].astype(BF16).astype(F32)
            delta = column_sum(part * ctxt_ref[s, lo : lo + HEAD, :].astype(F32)) * inv
            high = delta.astype(BF16).astype(F32)
            low = delta - high
            row = lax.broadcasted_iota(jnp.int32, (HEAD, length), 0)
            feat = jnp.where(row == 0, -high, jnp.where(row == 1, -low, 0.0))
            part = part * inv
            da_s[h, :HEAD, :] = part.astype(BF16)
            da_s[h, HEAD:, :] = feat.astype(BF16)
            dcx_s[h] = jnp.transpose(part).astype(BF16)

    def back_head(s, h):
        j = s * heads + h
        slot = j % 2
        fetch(j, slot).wait()
        for t0, n in spans:
            dp_t = nn(va[s, h], da_s[h, :, t0 : t0 + n])
            ds = (es[slot, :, t0 : t0 + n].astype(F32) * dp_t).astype(BF16)
            ds_s[:, t0 : t0 + n] = ds
            ct_s[rows_at(h, HEAD), t0 : t0 + n] = tn(ka[s, h, :, :HEAD], ds) * 0.125
        dv_s[h] = nn(es[slot], dcx_s[h]).astype(BF16)
        dk_s[h] = nn(ds_s[...], qa[s, h, :, :HEAD]).astype(BF16)
        if j + 2 < seqs * heads:
            fetch(j + 2, slot).start()

    def back_end(s):
        dq_s[0] = jnp.transpose(ct_s[...]).astype(BF16)
        dq_s[1] = jnp.concatenate([dk_s[h] for h in range(heads)], axis=1)
        dq_s[2] = jnp.concatenate([dv_s[h] for h in range(heads)], axis=1)

        def rows_out(dst, base):
            def body(i):
                r = rows_at(i, BLOCK, base)
                p = nt(dq_s[0, r, :], w_ref[0]) + nt(dq_s[1, r, :], w_ref[1]) + nt(dq_s[2, r, :], w_ref[2])
                dst[rows_at(i, BLOCK), :] = p.astype(BF16)

            loop(half // BLOCK, body)

        rows_out(send.at[s], other)
        pair_g[s].start()
        rows_out(mine.at[s], own)

    def back_grads(s):
        for i in (2, 3, 0, 1):
            p = tn(dq_s[i], h1_ref[s]) if i < 3 else nn(ctxt_ref[s], dxs[...])
            r = slice(i * local, (i + 1) * local)
            if s > 0:
                p = p + gbuf[2, r, :].astype(F32)
            gbuf[2, r, :] = p.astype(BF16)
        add_sum(7, column_sum(dq_s[0].astype(F32)))
        sv[8:9, :local] += column_sum(dq_s[2].astype(F32))

    def place(k, stage, dst_h, s):
        rows = pl.ds(pl.multiple_of(s * length + own, 16), half)
        here = pltpu.make_async_copy(stage, dst_h.at[rows], out_sem.at[k, 0])
        there = remote(stage, dst_h.at[rows], out_sem.at[k, 1], out_sem.at[k, 2], "tensor", core)
        here.start()
        there.start()
        return here, there

    def layer_out(s):
        pair_m[s].finish()
        b3 = shift_ref[3:4, :].astype(F32)
        stage = send.at[2 * seqs]

        def body(i):
            r = rows_at(i, BLOCK)
            stage[r, :] = (x1_ref[s, r, :] + pair_m[s].total(r) + b3).astype(BF16)

        loop(half // BLOCK, body)
        return place(s, stage, out_h, s)

    def input_grad(s):
        pair_g[s].finish()
        g = gain_ref[0:1, :].astype(F32)
        stage = send.at[s]

        def body(i):
            r = rows_at(i, BLOCK)
            dh1 = pair_g[s].total(r)
            scaled, factor = normalize(tok[rows_at(i, BLOCK, s * length + own), :].astype(F32))
            stage[r, :] = (dx_ref[s, r, :] + norm_back(dh1, scaled, factor, g)).astype(BF16)
            add_sum(0, column_sum(dh1 * scaled))
            add_sum(2, column_sum(dh1))

        loop(half // BLOCK, body)
        return place(seqs + s, stage, grad_h, s)

    def small_job():
        sem = iter(range(small_sem.shape[0]))
        two = lambda: (small_sem.at[next(sem)], small_sem.at[next(sem)])
        slot = iter(range(svr.shape[0]))
        k = next(slot)
        cp = remote(sv.at[pl.ds(0, 6)], svr.at[k, pl.ds(0, 6)], *two(), "tensor", core)
        cp.start()
        yield
        cp.wait()
        sv[0:6, :] += svr[k, 0:6, :]
        for p in [xpeer]:
            k = next(slot)
            cp = remote(sv, svr.at[k], *two(), "dp", p)
            cp.start()
            yield
            cp.wait()
            sv[...] += svr[k]
        base = k + 1
        cps = []
        for i, p in enumerate(zpeers):
            cps.append(remote(sv, svr.at[base + zi], *two(), "dp", p))
        for cp in cps:
            cp.start()
        svr[base + zi] = sv[...]
        yield
        for cp in cps:
            cp.wait()
        total = svr[base]
        for i in range(1, group):
            total = total + svr[base + i]
        sv[...] = total
        for i, p in enumerate(epeers):
            k = base + group + i
            cp = remote(sv, svr.at[k], *two(), "dp", p)
            cp.start()
            yield
            cp.wait()
            sv[...] += svr[k]
        small_ref[...] = sv[...]

    load_tok0.wait()
    load_w.wait()
    project(0)
    load_ow.wait()
    attend(0)
    load_tok1.wait()
    for s in range(1, seqs):
        project(s)
        pair_a[s - 1].middle()
        attend(s)
    load_fc1.wait()
    load_cot.wait()
    load_fc2.wait()
    pair_a[seqs - 1].middle()
    for k in (seqs * heads - 2, seqs * heads - 1):
        spill(k, k % 2).wait()
    for k in (0, 1):
        fetch(k, k % 2).start()
    jobs = []
    for s in range(seqs):
        norm_two(s)
        feed_forward(s, own, mine.at[2 * seqs + s], mine.at[seqs + s])
        h2_copies[s].wait()
        feed_forward(s, other, send.at[2 * seqs], send.at[seqs + s])
        pair_d[s].start()
        pair_m[s].start()
        fc2_grad(s)
        pair_d[s].middle()
        if s == seqs - 1:
            jobs += [reduce_job(0, ch) for ch in range(CHUNKS)]
            advance(*jobs)
        pair_m[s].gather()
        fc1_grad(s)
    jobs += [reduce_job(1, ch) for ch in range(CHUNKS)]
    advance(*jobs)
    for s in range(seqs):
        mid(s)
        pair_m[s].to_chip.start()
        back_setup(s)
        for h in range(heads):
            back_head(s, h)
            advance(*jobs)
        back_end(s)
        back_grads(s)
        pair_g[s].middle()
    jobs += [reduce_job(2, ch) for ch in reversed(range(CHUNKS))]
    advance(*jobs)
    copies = []
    for s in range(seqs):
        done = layer_out(s)
        advance(*jobs)
        if s < seqs - 1:
            for cp in done:
                cp.wait()
        else:
            copies += done
    for s in range(seqs):
        copies += input_grad(s)
        advance(*jobs)
    jobs.append(small_job())
    drain(*jobs)
    for cp in copies:
        cp.wait()


def struct(shape, dtype):
    return jax.ShapeDtypeStruct(shape, dtype)


def layer(n_dp, starts, marks, gains, shifts, qvb, b1, tokens, cot, w, ow, fc1, fc2):
    rows, width = tokens.shape
    seqs = starts.shape[0]
    length = rows // seqs
    half = length // 2
    local = w.shape[2]
    heads = local // HEAD
    hidden = fc1.shape[1]
    group = min(4, n_dp // 2)
    extra = (n_dp // (2 * group)).bit_length() - 1
    matrix = 4 * local
    part = matrix // CHUNKS // 2
    piece = part // group
    jobs = 3 * CHUNKS
    smem = pl.BlockSpec(memory_space=pltpu.SMEM)
    vmem = pl.BlockSpec(memory_space=pltpu.VMEM)
    hbm = pl.BlockSpec(memory_space=pl.ANY)
    v = pltpu.VMEM
    dma = pltpu.SemaphoreType.DMA
    small = 9
    return pl.pallas_call(
        functools.partial(layer_kernel, seqs, length, heads, n_dp, group, extra),
        in_specs=[smem, smem, vmem, vmem, vmem, vmem] + [hbm] * 6,
        out_specs=[hbm, hbm, hbm, vmem, hbm],
        scratch_shapes=[
            v((rows, width), BF16),
            v((rows, width), BF16),
            v(w.shape, BF16),
            v(ow.shape, BF16),
            v(fc1.shape, BF16),
            v(fc2.shape, BF16),
            v((seqs, length, width), BF16),
            v((seqs, heads, length, 2 * HEAD), BF16),
            v((seqs, heads, length, 2 * HEAD), BF16),
            v((seqs, heads, length, 2 * HEAD), BF16),
            v((2, length, length), BF16),
            v((2, length, 256), F32),
            v((local, length), F32),
            v((seqs, local, length), BF16),
            v((seqs, heads, 8, length), F32),
            v((2 * seqs + 1, half, width), BF16),
            v((3 * seqs, half, width), BF16),
            v((2 * seqs + 1, half, width), BF16),
            v((3 * seqs, half, width), BF16),
            v((seqs, half, width), F32),
            v((seqs, half, width), F32),
            v((seqs, length, width), BF16),
            v((length, width), BF16),
            v((seqs, half, width), BF16),
            v((seqs, half, width), BF16),
            v((length, length), BF16),
            v((heads, 2 * HEAD, length), BF16),
            v((heads, length, HEAD), BF16),
            v((3, length, local), BF16),
            v((heads, length, HEAD), BF16),
            v((heads, length, HEAD), BF16),
            v((3, matrix, width), BF16),
            v((jobs, part, width), BF16),
            v((jobs, group - 1, piece, width), BF16),
            v((jobs, max(extra, 1), piece, width), BF16),
            v((small, width), F32),
            v((2 + group + extra, small, width), F32),
            dma((7,)),
            dma((4,)),
            dma((4 * seqs, 4)),
            dma((seqs, 2)),
            dma((seqs, 2)),
            dma((jobs, 5 + 4 * (group - 1) + 2 * extra)),
            dma((2 * seqs, 3)),
            dma((4 + 2 * (group - 1) + 2 * extra,)),
        ],
        out_shape=[
            struct((rows, width), BF16),
            struct((rows, width), BF16),
            struct((3, matrix, width), BF16),
            struct((small, width), F32),
            struct((seqs * heads, length, length), BF16),
        ],
        compiler_params=pltpu.CompilerParams(
            collective_id=1, has_side_effects=True, vmem_limit_bytes=63 * 1024 * 1024
        ),
        name="layer",
        cost_estimate=pl.CostEstimate(flops=24 * 10**9, bytes_accessed=50 * 10**6, transcendentals=8 * 10**6),
    )(starts, marks, gains, shifts, qvb, b1, tokens, cot, w, ow, fc1, fc2)


def shards(
    n_dp, tokens, clip_starts, cls_index, norm_gains, shifts, qkv_weight, qv_bias,
    out_weight, fc1_weight, fc1_bias, fc2_weight, cotangent,
):
    width = tokens.shape[1]
    local = qv_bias.shape[1]
    w = jnp.transpose(qkv_weight, (1, 0, 2))
    layer_out, input_grad, mats, small, _ = layer(
        n_dp, clip_starts, cls_index, norm_gains, shifts, qv_bias, fc1_bias.reshape(1, -1), tokens, cotangent,
        w, out_weight, fc1_weight, fc2_weight,
    )
    attn = mats[2].astype(F32).reshape(4, local, width)
    return (
        layer_out,
        input_grad,
        small[0:2],
        small[2:6],
        jnp.transpose(attn[:3], (2, 0, 1)),
        small[7:9, :local],
        attn[3],
        mats[1].astype(F32),
        small[6],
        mats[0].astype(F32),
    )


def solution(mesh):
    row = P("dp", None)
    return jax.shard_map(
        functools.partial(shards, mesh.shape["dp"]),
        mesh=mesh,
        in_specs=(
            row,
            row,
            row,
            P(),
            P(),
            P(None, None, "tensor"),
            P(None, "tensor"),
            P("tensor", None),
            P(None, "tensor"),
            P("tensor"),
            P("tensor", None),
            row,
        ),
        out_specs=(
            row,
            row,
            P(),
            P(),
            P(None, None, "tensor"),
            P(None, "tensor"),
            P("tensor", None),
            P(None, "tensor"),
            P("tensor"),
            P("tensor", None),
        ),
        check_vma=False,
    )
```

time: 829 us -> 232 us (0.28)
  waiting for transfers between devices: 448 us -> 0 us
  Pallas kernels: 0 us -> 210 us
  matrix products: 149 us -> 0 us
  other arithmetic: 93.2 us -> 4.62 us
  blocking collectives: 64.6 us -> 0 us
  local copies, waits for them, and re-layouts: 50 us -> 15.4 us
  between operations: 15 us -> 0.66 us
    psum x3 -> x0, waiting for transfers between devices: 350 us -> none  [the longest x1 180 us: shards(): lax.psum((qkv_grad, qv_bias_grad, out_grad, fc1_grad, fc1_bias_grad, fc2_...]
    pallas_call x0 -> x1, Pallas kernels: none -> 210 us  [layer(): pl.pallas_call(functools.partial(layer_kernel, seqs, length, heads, n_dp,...]
    dot_general x29 -> x0, matrix products: 143 us -> none  [the longest x6 31.9 us: raw_scores(): jnp.einsum('qhd,khd->hqk', queries, key_rows, preferred_element_type=jnp....]
    reduce_scatter x2 -> x0, waiting for transfers between devices: 71.1 us -> none  [the longest x1 35.6 us: shards(): lax.psum_scatter(contract_cols(row_block, fc1_weight).astype(jnp.bfloat16...]
    psum x2 -> x0, blocking collectives: 64.6 us -> none  [the longest x1 44.9 us: shards(): lax.psum((gain_part, shift_part), ('dp', 'tensor'))]
    sub x3 -> x0, other arithmetic: 29.3 us -> none  [the longest x2 29.3 us: attend(): exponent = jnp.exp(scores - row_max)]
    reduce_sum x12 -> x0, other arithmetic: 27.9 us -> none  [the longest x2 8.21 us: normalize(): jnp.mean(centre * centre, axis=-1, keepdims=True) + 1e-06]
    all_gather x2 -> x0, waiting for transfers between devices: 26.4 us -> none  [the longest x1 26.4 us: shards(): lax.all_gather(mid_own.astype(jnp.bfloat16), 'tensor', axis=0, tiled=True)]
  transfers between devices with their start and end apart: 7 -> 0, of which waited for: 6 -> 0; matrix products, arithmetic and copies ran while one was open for 3% -> 0% of each run, Pallas kernels for 0% -> 0%
where the time goes in v1:
time: 232 us; the launch traced here: 230 us
  Pallas kernels  210 us (91%)
  local copies, waits for them, and re-layouts  15.4 us (7%)
  other arithmetic  4.62 us (2%)
    pallas_call x1, Pallas kernels, layer(): pl.pallas_call(functools.partial(layer_kernel, seqs, length, heads, n_dp,...  210 us
    unnamed x7, local copies, waits for them, and re-layouts  6.63 us

profile of v1, /device:TPU:8, one launch (start us, length us, event | category | flops | bytes accessed | tf_op | source)
XLA Modules:
  0.0 230.2 jit_solution(8938328662431070821)
XLA Ops:
  0.6 1.3 reshape.35.b1_ref
  1.9 2.3 %copy.22 = bf16[768,3,192]{2,0,1:T(8,128)(2,1)} copy(bf16[768,3,192]{0,2,1:T(8,128)(2,1)} %param.17) | data formatting | bytes 1769472 | tf_op args[5]
  4.2 209.5 %layer.1 = (bf16[1792,768]{1,0:T(8,128)(2,1)}, bf16[1792,768]{1,0:T(8,128)(2,1)}, bf16[3,768,768]{2,1,0:T(8,128)(2,1)}, f32[9,768]{1,0:T(8,128)}, bf16[6,896,896]{2,1,0:T(8,128)(2,1)}) custom-call(s32[2,4]{1,0:T(2,128)} %st_ref.1, s32[2,4]{1,0:T(2,128)} %mk_ref.1, bf16[2,768]{1,0:T(2,128)(2,1)} %gain_ref.1, bf16[4,768]{1,0:T(4,128)(2,1)} %shift_ref.1, ...), custom_call_target="tpu_custom_call" | custom-call | flops 24000000000 | bytes 50000000 | tf_op jit(solution)/shard_map/layer/pallas_call | solution.py:625
  213.7 1.3 slice.40
  215.0 1.3 slice_reduce_fusion
  216.4 1.3 slice.35
  217.7 1.3 slice.36
  219.1 4.6 %bitcast_convert_fusion = (f32[768,768]{1,0:T(8,128)}, f32[768,768]{1,0:T(8,128)}, f32[1,768,768]{2,1,0:T(8,128)S(1)}) fusion(bf16[3,768,768]{2,1,0:T(8,128)(2,1)} %get-tuple-element.17), kind=kLoop, calls=%fused_computation | loop fusion | flops 1769472 | bytes 10616832 | tf_op jit(solution)/shard_map/convert_element_type | solution.py:713
  223.7 0.0 copy-start.1
  223.7 0.9 slice_bitcast_fusion
  224.5 1.3 slice.46
  225.8 0.0 copy-done.1
  225.9 0.0 copy-start
  225.9 1.5 copy.25
  227.4 1.2 copy-done
  228.6 1.5 copy.26
Async XLA Ops:
  223.7 2.2 copy-start.1
  225.9 2.8 %copy-start = (bf16[1792,768]{1,0:T(8,128)(2,1)S(1)}, bf16[1792,768]{1,0:T(8,128)(2,1)}, u32[]{:S(2)}) copy-start(bf16[1792,768]{1,0:T(8,128)(2,1)} %get-tuple-element.32) | copy-start | bytes 8257540

commit v2 on v1

--- a/solution.py
+++ b/solution.py
@@ -12,7 +12,10 @@
 F32 = jnp.float32
 BF16 = jnp.bfloat16
 BLOCK = 112
-CHUNKS = 2
+ROW_CHUNKS = 2
+COLUMN_CHUNKS = 1
+CHUNKS = ROW_CHUNKS * COLUMN_CHUNKS
+TICKS = (1, 0, 1, 1, 1, 1, 2, 1, 1, 1, 3, 2, 3, 3)
 MESH = pl.DeviceIdType.MESH
 
 
@@ -91,13 +94,42 @@
         return self.mine[r, :].astype(F32) + self.from_chip[r, :].astype(F32)
 
 
+class Links:
+    def __init__(self):
+        self.ready, self.flying = ([], []), ([], [])
+        self.turn = 0
+
+    def add(self, *jobs):
+        for job in jobs:
+            axis = next(job, None)
+            if axis is not None:
+                self.ready[axis].append(job)
+        self.fill()
+
+    def fill(self):
+        for axis in (0, 1):
+            while self.ready[axis] and len(self.flying[axis]) < 2:
+                job = self.ready[axis].pop(0)
+                next(job)
+                self.flying[axis].append(job)
+
+    def tick(self, times=1):
+        for _ in range(times):
+            axis = self.turn if self.flying[self.turn] else 1 - self.turn
+            if not self.flying[axis]:
+                return False
+            self.turn = 1 - axis
+            self.add(self.flying[axis].pop(0))
+        return True
+
+
 def layer_kernel(
     seqs, length, heads, n_dp, group, extra,
     st_ref, mk_ref, gain_ref, shift_ref, qvb_ref, b1_ref, tok_h, cot_h, w_h, ow_h, fc1_h, fc2_h,
     out_h, grad_h, gmat_h, small_ref, e_h,
-    tok, cot, w_ref, ow_ref, fc1, fc2, h1_ref, qa, ka, va, es, st_s, ct_s, ctxt_ref, linv_ref,
-    send, mine, fcore, fchip, x1_ref, dx_ref, h2_ref, dxs, dxr_mine, dxr_other, ds_s, da_s, dcx_s, dq_s,
-    dk_s, dv_s, gbuf, rx, rz, re, sv, svr,
+    tok, cot, ow_ref, fc1, fc2, h1_ref, qa, ka, va, es, ct_s, ctxt_ref, linv_ref,
+    bank, fcore, fchip, x1_ref, dx_ref, h2_ref, dxs, dxr_mine, dxr_other, ds_s, da_s, dcx_s, dq_s,
+    wt_s, gbuf, rx, rz, re, sv, svr,
     load_sem, e_sem, pair_sem, h2_sem, dx_sem, red_sem, out_sem, small_sem,
 ):
     half = length // 2
@@ -126,7 +158,7 @@
 
     tok_rows = [pl.ds(s * length, length) for s in range(seqs)]
     load_tok0 = load(0, tok_h.at[tok_rows[0]], tok.at[tok_rows[0]])
-    load_w = load(1, w_h, w_ref)
+    load_w = load(1, w_h, wt_s)
     load_tok1 = load(2, tok_h.at[pl.ds(length, (seqs - 1) * length)], tok.at[pl.ds(length, (seqs - 1) * length)])
     load_ow = load(3, ow_h, ow_ref)
     load_fc1 = load(4, fc1_h, fc1)
@@ -140,16 +172,18 @@
         pl.semaphore_signal(barrier, inc=1, device_id={"dp": peer}, device_id_type=MESH)
     pl.semaphore_wait(barrier, 3 + len(zpeers) + len(epeers))
 
-    def pair(b, q):
-        return Pair(send.at[b], mine.at[q], fcore.at[b], fchip.at[q], pair_sem.at[q], core, chip)
-
-    pair_a = [pair(s, s) for s in range(seqs)]
-    pair_d = [pair(seqs + s, seqs + s) for s in range(seqs)]
-    pair_m = [pair(2 * seqs, 2 * seqs + s) for s in range(seqs)]
-    pair_g = [
-        Pair(send.at[s], mine.at[s], fcore.at[s], fchip.at[s], pair_sem.at[3 * seqs + s], core, chip)
-        for s in range(seqs)
-    ]
+    send_a, mine_a, send_d, mine_d, mine_m = (list(range(k * seqs, (k + 1) * seqs)) for k in range(5))
+    send_m = [5 * seqs] * seqs
+
+    def pair(give, keep, core_slot, chip_slot, sem):
+        return Pair(
+            bank.at[give], bank.at[keep], fcore.at[core_slot], fchip.at[chip_slot], pair_sem.at[sem], core, chip
+        )
+
+    pair_a = [pair(send_a[s], mine_a[s], s, s, s) for s in range(seqs)]
+    pair_d = [pair(send_d[s], mine_d[s], seqs + s, seqs + s, seqs + s) for s in range(seqs)]
+    pair_m = [pair(send_m[s], mine_m[s], 2 * seqs, 2 * seqs + s, 2 * seqs + s) for s in range(seqs)]
+    pair_g = [pair(send_a[s], mine_a[s], s, s, 3 * seqs + s) for s in range(seqs)]
 
     sv[...] = jnp.zeros_like(sv)
 
@@ -168,20 +202,25 @@
         qvb = qvb_ref[...].astype(F32)
         size = 128
 
-        def body(i):
-            r = rows_at(i, size)
+        def norm(i):
             x = tok[rows_at(i, size, s * length), :].astype(F32)
             scaled, _ = normalize(x)
-            h1 = (scaled * gain + shift).astype(BF16)
-            h1_ref[s, r, :] = h1
-            q = (nn(h1, w_ref[0]) + qvb[0:1]).astype(BF16).astype(F32) * 0.125
+            h1_ref[s, rows_at(i, size), :] = (scaled * gain + shift).astype(BF16)
+
+        loop(length // size, norm)
+        block = half
+
+        def body(i):
+            r = rows_at(i, block)
+            h1 = h1_ref[s, r, :]
+            q = (nt(h1, wt_s[:local]) + qvb[0:1]).astype(BF16).astype(F32) * 0.125
             q = q.astype(BF16)
-            k = nn(h1, w_ref[1]).astype(BF16)
-            v = (nn(h1, w_ref[2]) + qvb[1:2]).astype(BF16)
-            pos = lax.broadcasted_iota(jnp.int32, (size, HEAD), 0) + i * size
-            lane = lax.broadcasted_iota(jnp.int32, (size, HEAD), 1)
-            clip = jnp.zeros((size, HEAD), jnp.int32) - 1
-            mark = jnp.zeros((size, HEAD), jnp.int32)
+            k = nt(h1, wt_s[local : 2 * local]).astype(BF16)
+            v = (nt(h1, wt_s[2 * local :]) + qvb[1:2]).astype(BF16)
+            pos = lax.broadcasted_iota(jnp.int32, (block, HEAD), 0) + i * block
+            lane = lax.broadcasted_iota(jnp.int32, (block, HEAD), 1)
+            clip = jnp.zeros((block, HEAD), jnp.int32) - 1
+            mark = jnp.zeros((block, HEAD), jnp.int32)
             for n in range(clips):
                 clip = clip + jnp.where(pos >= st_ref[s, n], 1, 0)
                 mark = mark + jnp.where(pos == mk_ref[s, n], 1, 0)
@@ -195,7 +234,7 @@
                 ka[s, h, r, :] = jnp.concatenate([k[:, cols], kf], axis=1)
                 va[s, h, r, :] = jnp.concatenate([v[:, cols], vf], axis=1)
 
-        loop(length // size, body)
+        loop(length // block, body)
 
     spans = [(t0, min(256, length - t0)) for t0 in range(0, length, 256)]
 
@@ -211,16 +250,19 @@
             v = va[s, h, :, :HEAD]
             for i, (t0, n) in enumerate(spans):
                 sl = i % 2
-                st_s[sl, :, :n] = nt(ka[s, h], qa[s, h, t0 : t0 + n])
+                score = nt(ka[s, h], qa[s, h, t0 : t0 + n])
+                dx_ref[sl, :, :n] = score[:half]
+                dx_ref[sl, :, 256 : 256 + n] = score[half:]
+                scores = lambda u, ch: dx_ref[sl, u % half : u % half + ch, (u // half) * 256 : (u // half) * 256 + n]
                 ch = 64
                 m = None
                 for u in range(0, length, ch):
-                    x = jnp.max(st_s[sl, u : u + ch, :n].reshape(ch // 8, 8, n), axis=0)
+                    x = jnp.max(scores(u, ch).reshape(ch // 8, 8, n), axis=0)
                     m = x if m is None else jnp.maximum(m, x)
                 m = jnp.max(m, axis=0, keepdims=True)
                 tot = None
                 for u in range(0, length, ch):
-                    x = jnp.exp(st_s[sl, u : u + ch, :n] - m)
+                    x = jnp.exp(scores(u, ch) - m)
                     es[slot, u : u + ch, t0 : t0 + n] = x.astype(BF16)
                     x = jnp.sum(x.reshape(ch // 8, 8, n), axis=0)
                     tot = x if tot is None else tot + x
@@ -231,17 +273,14 @@
 
         loop(heads, head)
         ctxt_ref[s] = ct_s[...].astype(BF16)
-        dq_s[0] = jnp.transpose(ct_s[...]).astype(BF16)
+        dq_s[:, :local] = jnp.transpose(ct_s[...]).astype(BF16)
 
         def rows_out(dst, base):
-            def body(i):
-                dst[rows_at(i, BLOCK), :] = nn(dq_s[0, rows_at(i, BLOCK, base), :], ow_ref[...]).astype(BF16)
-
-            loop(half // BLOCK, body)
-
-        rows_out(send.at[s], other)
+            bank[dst] = nn(dq_s[pl.ds(base, half), :local], ow_ref[...]).astype(BF16)
+
+        rows_out(send_a[s], other)
         pair_a[s].start()
-        rows_out(mine.at[s], own)
+        rows_out(mine_a[s], own)
 
     h2_copies = [
         remote(
@@ -270,24 +309,51 @@
 
     act_ref, dpre_ref = ds_s, dxs
 
-    def feed_forward(s, base, mlp_dst, dh2_dst):
-        size = BLOCK
-
-        def body(i):
-            r = rows_at(i, size, base)
-            pre = nn(h2_ref[s, r, :], fc1[...]) + b1_ref[...].astype(F32)
+    def feed_forward(s):
+        size = half // 2
+        n = length // size
+        b1 = b1_ref[...].astype(F32).reshape(1, hidden)
+        at = lambda i: own + (i // 2) * (other - own) + (i % 2) * size
+        rows = lambda i, base=0: pl.ds(pl.multiple_of(base + at(i), 16), size)
+
+        def first(i):
+            dx_ref[i % 2, :size, :] = nn(h2_ref[s, rows(i), :], fc1[...]) + b1
+
+        def second(i):
+            dact = nt(cot[rows(i, s * length), :], fc2[...])
+            pre = dx_ref[i % 2, :size, :]
             phi = 0.5 * (1.0 + lax.erf(pre * 0.7071067811865476))
-            act = (pre * phi).astype(BF16)
-            act_ref[r, :hidden] = act
+            act_ref[rows(i), :hidden] = (pre * phi).astype(BF16)
             slope = phi + pre * (0.3989422804014327 * jnp.exp(-0.5 * pre * pre))
-            dact = nt(cot[rows_at(i, size, s * length + base), :], fc2[...])
             dpre = (dact * slope).astype(BF16)
-            dpre_ref[r, :hidden] = dpre
+            dpre_ref[rows(i), :hidden] = dpre
             add_sum(6, column_sum(dpre.astype(F32)))
-            dh2_dst[rows_at(i, size), :] = nt(dpre, fc1[...]).astype(BF16)
-            mlp_dst[rows_at(i, size), :] = nn(act, fc2[...]).astype(BF16)
-
-        loop(half // size, body)
+
+        def third(i):
+            far = i // 2
+            r = pl.ds(pl.multiple_of((i % 2) * size, size), size)
+            bank[mine_m[s] + far * (send_m[s] - mine_m[s]), r, :] = nn(act_ref[rows(i), :hidden], fc2[...]).astype(BF16)
+            bank[mine_d[s] + far * (send_d[s] - mine_d[s]), r, :] = nt(dpre_ref[rows(i), :hidden], fc1[...]).astype(BF16)
+
+        first(0)
+        first(1)
+        second(0)
+
+        def body(k):
+            i = k + 1
+
+            @pl.when(k == 0)
+            def _():
+                h2_copies[s].wait()
+
+            third(i - 1)
+            first(i + 1)
+            second(i)
+
+        loop(n - 2, body)
+        third(n - 2)
+        second(n - 1)
+        third(n - 1)
 
     def fc_grad(m, left, right, s, tile):
         def body(i):
@@ -305,30 +371,33 @@
     def fc1_grad(s):
         fc_grad(1, lambda r: h2_ref[s, :, r], lambda: dpre_ref[:, :hidden], s, 256)
 
-    piece = gbuf.shape[1] // CHUNKS // 2 // group
+    piece = gbuf.shape[1] // ROW_CHUNKS // 2 // group
+    span = width // COLUMN_CHUNKS
 
     def reduce_job(m, ch):
         job = m * CHUNKS + ch
-        base = ch * (gbuf.shape[1] // CHUNKS)
+        base = (ch // COLUMN_CHUNKS) * (gbuf.shape[1] // ROW_CHUNKS)
+        cols = pl.ds((ch % COLUMN_CHUNKS) * span, span)
         part = group * piece
         sem = iter(range(red_sem.shape[1]))
         two = lambda: (red_sem.at[job, next(sem)], red_sem.at[job, next(sem)])
-        rows = lambda start, n: gbuf.at[m, pl.ds(pl.multiple_of(start, 16), n)]
+        rows = lambda start, n: gbuf.at[m, pl.ds(pl.multiple_of(start, 16), n), cols]
 
         def add(start, n, sources):
             size = piece
 
             def body(i):
                 r = rows_at(i, size, start)
-                total = gbuf[m, r, :].astype(F32)
+                total = gbuf[m, r, cols].astype(F32)
                 for src in sources:
                     total = total + src[rows_at(i, size), :].astype(F32)
-                gbuf[m, r, :] = total.astype(BF16)
+                gbuf[m, r, cols] = total.astype(BF16)
 
             loop(n // size, body)
 
         mine_at = base + xi * part
         cp = remote(rows(base + (1 - xi) * part, part), rx.at[job], *two(), "dp", xpeer)
+        yield 0
         cp.start()
         yield
         cp.wait()
@@ -337,6 +406,7 @@
             remote(rows(mine_at + ((zi + k + 1) % group) * piece, piece), rz.at[job, k], *two(), "dp", p)
             for k, p in enumerate(zpeers)
         ]
+        yield 1
         for cp in cps:
             cp.start()
         yield
@@ -346,31 +416,27 @@
         add(piece_at, piece, [rz.at[job, k] for k in range(group - 1)])
         for k, p in enumerate(epeers):
             cp = remote(rows(piece_at, piece), re.at[job, k], *two(), "dp", p)
+            yield 1
             cp.start()
             yield
             cp.wait()
             add(piece_at, piece, [re.at[job, k]])
-        done = lambda start, n: gmat_h.at[m, pl.ds(pl.multiple_of(start, 16), n)]
+        done = lambda start, n: gmat_h.at[m, pl.ds(pl.multiple_of(start, 16), n), cols]
         cps = [remote(rows(piece_at, piece), done(piece_at, piece), *two(), "dp", p) for p in zpeers]
         cps.append(pltpu.make_async_copy(rows(piece_at, piece), done(piece_at, piece), red_sem.at[job, next(sem)]))
+        yield 1
         for cp in cps:
             cp.start()
         yield
         for cp in cps:
             cp.wait()
         cp = remote(done(mine_at, part), done(mine_at, part), *two(), "dp", xpeer)
+        yield 0
         cp.start()
         yield
         cp.wait()
 
-    def advance(*jobs):
-        for job in jobs:
-            next(job, None)
-
-    def drain(*jobs):
-        live = list(jobs)
-        while live:
-            live = [job for job in live if next(job, live) is not live]
+    links = Links()
 
     dx_copies = [
         remote(dxr_mine.at[s], dxr_other.at[s], dx_sem.at[s, 0], dx_sem.at[s, 1], "tensor", core)
@@ -425,37 +491,32 @@
             ds = (es[slot, :, t0 : t0 + n].astype(F32) * dp_t).astype(BF16)
             ds_s[:, t0 : t0 + n] = ds
             ct_s[rows_at(h, HEAD), t0 : t0 + n] = tn(ka[s, h, :, :HEAD], ds) * 0.125
-        dv_s[h] = nn(es[slot], dcx_s[h]).astype(BF16)
-        dk_s[h] = nn(ds_s[...], qa[s, h, :, :HEAD]).astype(BF16)
+        lo = h * HEAD
+        dq_s[:, 2 * local + lo : 2 * local + lo + HEAD] = nn(es[slot], dcx_s[h]).astype(BF16)
+        dq_s[:, local + lo : local + lo + HEAD] = nn(ds_s[...], qa[s, h, :, :HEAD]).astype(BF16)
         if j + 2 < seqs * heads:
             fetch(j + 2, slot).start()
 
     def back_end(s):
-        dq_s[0] = jnp.transpose(ct_s[...]).astype(BF16)
-        dq_s[1] = jnp.concatenate([dk_s[h] for h in range(heads)], axis=1)
-        dq_s[2] = jnp.concatenate([dv_s[h] for h in range(heads)], axis=1)
+        dq_s[:, :local] = jnp.transpose(ct_s[...]).astype(BF16)
 
         def rows_out(dst, base):
-            def body(i):
-                r = rows_at(i, BLOCK, base)
-                p = nt(dq_s[0, r, :], w_ref[0]) + nt(dq_s[1, r, :], w_ref[1]) + nt(dq_s[2, r, :], w_ref[2])
-                dst[rows_at(i, BLOCK), :] = p.astype(BF16)
-
-            loop(half // BLOCK, body)
-
-        rows_out(send.at[s], other)
+            bank[dst] = nn(dq_s[pl.ds(base, half), : 3 * local], wt_s[...]).astype(BF16)
+
+        rows_out(send_a[s], other)
         pair_g[s].start()
-        rows_out(mine.at[s], own)
+        rows_out(mine_a[s], own)
 
     def back_grads(s):
+        h1 = h1_ref[s]
         for i in (2, 3, 0, 1):
-            p = tn(dq_s[i], h1_ref[s]) if i < 3 else nn(ctxt_ref[s], dxs[...])
+            p = tn(dq_s[:, i * local : (i + 1) * local], h1) if i < 3 else nn(ctxt_ref[s], dxs[...])
             r = slice(i * local, (i + 1) * local)
             if s > 0:
                 p = p + gbuf[2, r, :].astype(F32)
             gbuf[2, r, :] = p.astype(BF16)
-        add_sum(7, column_sum(dq_s[0].astype(F32)))
-        sv[8:9, :local] += column_sum(dq_s[2].astype(F32))
+        add_sum(7, column_sum(dq_s[:, :local].astype(F32)))
+        sv[8:9, :local] += column_sum(dq_s[:, 2 * local : 3 * local].astype(F32))
 
     def place(k, stage, dst_h, s):
         rows = pl.ds(pl.multiple_of(s * length + own, 16), half)
@@ -468,7 +529,7 @@
     def layer_out(s):
         pair_m[s].finish()
         b3 = shift_ref[3:4, :].astype(F32)
-        stage = send.at[2 * seqs]
+        stage = bank.at[send_m[s]]
 
         def body(i):
             r = rows_at(i, BLOCK)
@@ -480,7 +541,7 @@
     def input_grad(s):
         pair_g[s].finish()
         g = gain_ref[0:1, :].astype(F32)
-        stage = send.at[s]
+        stage = bank.at[send_a[s]]
 
         def body(i):
             r = rows_at(i, BLOCK)
@@ -551,49 +612,55 @@
         spill(k, k % 2).wait()
     for k in (0, 1):
         fetch(k, k % 2).start()
-    jobs = []
+    end = seqs - 1
     for s in range(seqs):
         norm_two(s)
-        feed_forward(s, own, mine.at[2 * seqs + s], mine.at[seqs + s])
-        h2_copies[s].wait()
-        feed_forward(s, other, send.at[2 * seqs], send.at[seqs + s])
+        feed_forward(s)
         pair_d[s].start()
         pair_m[s].start()
         fc2_grad(s)
         pair_d[s].middle()
-        if s == seqs - 1:
-            jobs += [reduce_job(0, ch) for ch in range(CHUNKS)]
-            advance(*jobs)
+        if s == end:
+            links.add(*[reduce_job(0, ch) for ch in range(CHUNKS)])
         pair_m[s].gather()
         fc1_grad(s)
-    jobs += [reduce_job(1, ch) for ch in range(CHUNKS)]
-    advance(*jobs)
+    links.add(*[reduce_job(1, ch) for ch in range(CHUNKS)])
+    tick = lambda k: links.tick(TICKS[k])
     for s in range(seqs):
+        last = int(s == end)
+        if s > 0:
+            tick(0)
         mid(s)
-        pair_m[s].to_chip.start()
+        tick(1 + last)
         back_setup(s)
         for h in range(heads):
             back_head(s, h)
-            advance(*jobs)
+            tick(3 + 3 * last + min(h, 2))
+            if h == 1:
+                pair_m[s].to_chip.start()
         back_end(s)
         back_grads(s)
         pair_g[s].middle()
-    jobs += [reduce_job(2, ch) for ch in reversed(range(CHUNKS))]
-    advance(*jobs)
+        if s == end:
+            links.add(*[reduce_job(2, ch) for ch in reversed(range(CHUNKS))])
+        tick(9 + last)
     copies = []
-    for s in range(seqs):
-        done = layer_out(s)
-        advance(*jobs)
-        if s < seqs - 1:
-            for cp in done:
-                cp.wait()
-        else:
-            copies += done
-    for s in range(seqs):
+    for s in range(end):
         copies += input_grad(s)
-        advance(*jobs)
-    jobs.append(small_job())
-    drain(*jobs)
+        tick(11)
+        for cp in layer_out(s):
+            cp.wait()
+        tick(12)
+    copies += input_grad(end)
+    small = small_job()
+    next(small)
+    tick(13)
+    next(small, None)
+    copies += layer_out(end)
+    while links.tick():
+        next(small, None)
+    for _ in small:
+        pass
     for cp in copies:
         cp.wait()
 
@@ -607,13 +674,14 @@
     seqs = starts.shape[0]
     length = rows // seqs
     half = length // 2
-    local = w.shape[2]
+    local = w.shape[0] // 3
     heads = local // HEAD
     hidden = fc1.shape[1]
     group = min(4, n_dp // 2)
     extra = (n_dp // (2 * group)).bit_length() - 1
     matrix = 4 * local
-    part = matrix // CHUNKS // 2
+    part = matrix // ROW_CHUNKS // 2
+    span = width // COLUMN_CHUNKS
     piece = part // group
     jobs = 3 * CHUNKS
     smem = pl.BlockSpec(memory_space=pltpu.SMEM)
@@ -629,7 +697,6 @@
         scratch_shapes=[
             v((rows, width), BF16),
             v((rows, width), BF16),
-            v(w.shape, BF16),
             v(ow.shape, BF16),
             v(fc1.shape, BF16),
             v(fc2.shape, BF16),
@@ -638,12 +705,10 @@
             v((seqs, heads, length, 2 * HEAD), BF16),
             v((seqs, heads, length, 2 * HEAD), BF16),
             v((2, length, length), BF16),
-            v((2, length, 256), F32),
             v((local, length), F32),
             v((seqs, local, length), BF16),
             v((seqs, heads, 8, length), F32),
-            v((2 * seqs + 1, half, width), BF16),
-            v((3 * seqs, half, width), BF16),
+            v((5 * seqs + 1, half, width), BF16),
             v((2 * seqs + 1, half, width), BF16),
             v((3 * seqs, half, width), BF16),
             v((seqs, half, width), F32),
@@ -655,13 +720,12 @@
             v((length, length), BF16),
             v((heads, 2 * HEAD, length), BF16),
             v((heads, length, HEAD), BF16),
-            v((3, length, local), BF16),
-            v((heads, length, HEAD), BF16),
-            v((heads, length, HEAD), BF16),
+            v((length, 3 * local), BF16),
+            v((3 * local, width), BF16),
             v((3, matrix, width), BF16),
-            v((jobs, part, width), BF16),
-            v((jobs, group - 1, piece, width), BF16),
-            v((jobs, max(extra, 1), piece, width), BF16),
+            v((jobs, part, span), BF16),
+            v((jobs, group - 1, piece, span), BF16),
+            v((jobs, max(extra, 1), piece, span), BF16),
             v((small, width), F32),
             v((2 + group + extra, small, width), F32),
             dma((7,)),
@@ -688,30 +752,85 @@
     )(starts, marks, gains, shifts, qvb, b1, tokens, cot, w, ow, fc1, fc2)
 
 
+def finish_kernel(
+    out_h, grad_h, mats_h, small_ref, out_o, grad_o, gain_o, shift_o, qkv_o, qvb_o, ow_o, fc1_o, b1_o, fc2_o,
+    low, wide, rows, load_sem, store_sem,
+):
+    local = qvb_o.shape[1]
+    loads = [pltpu.make_async_copy(mats_h.at[m], low.at[m], load_sem.at[m]) for m in range(3)]
+    for k, ref in enumerate((out_h, grad_h)):
+        loads.append(pltpu.make_async_copy(ref, rows.at[k], load_sem.at[3 + k]))
+    for cp in loads:
+        cp.start()
+    stores = []
+    gain_o[...] = small_ref[0:2, :]
+    shift_o[...] = small_ref[2:6, :]
+    b1_o[...] = small_ref[6, : b1_o.shape[0]]
+    qvb_o[...] = small_ref[7:9, :local]
+    targets = ([(fc2_o, 0, fc2_o.shape[0])], [(fc1_o, 0, fc1_o.shape[0])], [(qkv_o, 0, 3 * local), (ow_o, 3 * local, local)])
+    for m in range(3):
+        loads[m].wait()
+        wide[m] = low[m].astype(F32)
+        for k, (ref, start, n) in enumerate(targets[m]):
+            cp = pltpu.make_async_copy(wide.at[m, pl.ds(start, n)], ref, store_sem.at[2 + m + k])
+            cp.start()
+            stores.append(cp)
+    for k, ref in enumerate((out_o, grad_o)):
+        loads[3 + k].wait()
+        cp = pltpu.make_async_copy(rows.at[k], ref, store_sem.at[k])
+        cp.start()
+        stores.append(cp)
+    for cp in stores:
+        cp.wait()
+
+
+def finish(local, hidden, layer_out, input_grad, mats, small):
+    rows, width = layer_out.shape
+    vmem = pl.BlockSpec(memory_space=pltpu.VMEM)
+    hbm = pl.BlockSpec(memory_space=pltpu.HBM)
+    return pl.pallas_call(
+        finish_kernel,
+        in_specs=[hbm, hbm, hbm, vmem],
+        out_specs=[hbm, hbm, vmem, vmem, hbm, vmem, hbm, hbm, vmem, hbm],
+        scratch_shapes=[
+            pltpu.VMEM(mats.shape, BF16),
+            pltpu.VMEM(mats.shape, F32),
+            pltpu.VMEM((2, rows, width), BF16),
+            pltpu.SemaphoreType.DMA((5,)),
+            pltpu.SemaphoreType.DMA((6,)),
+        ],
+        out_shape=[
+            struct((rows, width), BF16),
+            struct((rows, width), BF16),
+            struct((2, width), F32),
+            struct((4, width), F32),
+            struct((3 * local, width), F32),
+            struct((2, local), F32),
+            struct((local, width), F32),
+            struct((width, hidden), F32),
+            struct((hidden,), F32),
+            struct((hidden, width), F32),
+        ],
+        compiler_params=pltpu.CompilerParams(vmem_limit_bytes=63 * 1024 * 1024),
+        name="finish",
+    )(layer_out, input_grad, mats, small)
+
+
 def shards(
     n_dp, tokens, clip_starts, cls_index, norm_gains, shifts, qkv_weight, qv_bias,
     out_weight, fc1_weight, fc1_bias, fc2_weight, cotangent,
 ):
     width = tokens.shape[1]
     local = qv_bias.shape[1]
-    w = jnp.transpose(qkv_weight, (1, 0, 2))
+    hidden = fc1_bias.shape[0]
+    w = jnp.transpose(qkv_weight, (1, 2, 0)).reshape(3 * local, width)
     layer_out, input_grad, mats, small, _ = layer(
-        n_dp, clip_starts, cls_index, norm_gains, shifts, qv_bias, fc1_bias.reshape(1, -1), tokens, cotangent,
+        n_dp, clip_starts, cls_index, norm_gains, shifts, qv_bias, fc1_bias, tokens, cotangent,
         w, out_weight, fc1_weight, fc2_weight,
     )
-    attn = mats[2].astype(F32).reshape(4, local, width)
-    return (
-        layer_out,
-        input_grad,
-        small[0:2],
-        small[2:6],
-        jnp.transpose(attn[:3], (2, 0, 1)),
-        small[7:9, :local],
-        attn[3],
-        mats[1].astype(F32),
-        small[6],
-        mats[0].astype(F32),
-    )
+    out, grad, gain, shift, qkv, qvb, ow, fc1, b1, fc2 = finish(local, hidden, layer_out, input_grad, mats, small)
+    qkv = jnp.transpose(qkv.reshape(3, local, width), (2, 0, 1))
+    return out, grad, gain, shift, qkv, qvb, ow, fc1, b1, fc2
 
 
 def solution(mesh):

time: 232 us -> 195 us (0.84)
  Pallas kernels: 210 us -> 190 us
  local copies, waits for them, and re-layouts: 15.4 us -> 0 us
  other arithmetic: 4.62 us -> 0 us
    pallas_call x1, Pallas kernels: 210 us -> 181 us  [layer(): pl.pallas_call(functools.partial(layer_kernel, seqs, length, heads, n_dp,...]
    pallas_call x0 -> x1, Pallas kernels: none -> 9.61 us  [finish(): pl.pallas_call(finish_kernel, in_specs=[hbm, hbm, hbm, vmem], out_specs=[...]
    slice x6 -> x0, local copies, waits for them, and re-layouts: 7.49 us -> none  [the longest x1 1.34 us: shards(): small[6]]
    unnamed x7 -> x0, local copies, waits for them, and re-layouts: 6.63 us -> none
    convert_element_type x1 -> x0, other arithmetic: 4.62 us -> none  [shards(): mats[0].astype(F32)]
where the time goes in v2:
time: 195 us; the launch traced here: 191 us
  Pallas kernels  190 us (97%)
    pallas_call x1, Pallas kernels, layer(): pl.pallas_call(functools.partial(layer_kernel, seqs, length, heads, n_dp,...  181 us
    pallas_call x1, Pallas kernels, finish(): pl.pallas_call(finish_kernel, in_specs=[hbm, hbm, hbm, vmem], out_specs=[...  9.61 us

profile of v2, /device:TPU:8, one launch (start us, length us, event | category | flops | bytes accessed | tf_op | source)
XLA Modules:
  0.0 191.1 jit_solution(7015717416676114498)
XLA Ops:
  0.6 180.6 %layer.1 = (bf16[1792,768]{1,0:T(8,128)(2,1)}, bf16[1792,768]{1,0:T(8,128)(2,1)}, bf16[3,768,768]{2,1,0:T(8,128)(2,1)}, f32[9,768]{1,0:T(8,128)}, bf16[6,896,896]{2,1,0:T(8,128)(2,1)}) custom-call(s32[2,4]{1,0:T(2,128)} %st_ref.1, s32[2,4]{1,0:T(2,128)} %mk_ref.1, bf16[2,768]{1,0:T(2,128)(2,1)} %gain_ref.1, bf16[4,768]{1,0:T(4,128)(2,1)} %shift_ref.1, ...), custom_call_target="tpu_custom_call" | custom-call | flops 24000000000 | bytes 50000000 | tf_op jit(solution)/shard_map/layer/pallas_call | solution.py:693
  181.3 9.6 %finish.1 = (bf16[1792,768]{1,0:T(8,128)(2,1)}, bf16[1792,768]{1,0:T(8,128)(2,1)}, f32[2,768]{1,0:T(2,128)}, f32[4,768]{1,0:T(4,128)}, f32[576,768]{1,0:T(8,128)...) custom-call(bf16[1792,768]{1,0:T(8,128)(2,1)} %get-tuple-element.24.out_, ...), custom_call_target="tpu_custom_call" | custom-call | tf_op jit(solution)/shard_map/finish/pallas_call | solution.py:791
